TPU v7x, 128 devices: a whole 4x4x4 slice. The times are simulated.
128 devices in a mesh: seq: 16 (over z, y), mp: 8 (over x, core).
Axes of the slice: x: 4, y: 4, z: 4, core: 2. Of those that a mesh axis runs over, the one named last changes fastest.
Arguments:
- tokens: bfloat16 [8192, 2048], P('seq'), may hold values from -6 to 6
- group_ids: int32 [8192], P('seq'), may hold values from 0 to 128, as said below
- gain_one: float32 [2048], replicated, may hold values from 0.5 to 1.5
- lin_query: bfloat16 [2048, 256], P(None, 'mp'), may hold values from -0.1875 to 0.1875
- lin_key: bfloat16 [2048, 256], P(None, 'mp'), may hold values from -0.1875 to 0.1875
- lin_value: bfloat16 [2048, 2048], P(None, 'mp'), may hold values from -0.125 to 0.125
- lin_output: bfloat16 [2048, 2048], P('mp'), may hold values from -0.5 to 0.5
- gain_two: float32 [2048], replicated, may hold values from 0.5 to 1.5
- win_query: bfloat16 [2048, 2048], P(None, 'mp'), may hold values from -0.125 to 0.125
- win_key: bfloat16 [2048, 2048], P(None, 'mp'), may hold values from -0.125 to 0.125
- win_value: bfloat16 [2048, 2048], P(None, 'mp'), may hold values from -0.125 to 0.125
- win_output: bfloat16 [2048, 2048], P('mp'), may hold values from -0.375 to 0.375
- gain_three: float32 [2048], replicated, may hold values from 0.5 to 1.5
- mlp_gate: bfloat16 [2048, 5632], P(None, 'mp'), may hold values from -0.125 to 0.125
- mlp_up: bfloat16 [2048, 5632], P(None, 'mp'), may hold values from -0.125 to 0.125
- mlp_down: bfloat16 [5632, 2048], P('mp'), may hold values from -0.078125 to 0.078125
- out_grad: bfloat16 [8192, 2048], P('seq'), may hold values from -6 to 6
Outputs:
- result: bfloat16 [8192, 2048], P('seq')
- tokens_grad: float32 [8192, 2048], P('seq')
- gain_one_grad: float32 [2048], P('seq')
- lin_query_grad: float32 [2048, 256], P('seq', 'mp')
- lin_key_grad: float32 [2048, 256], P('seq', 'mp')
- lin_value_grad: float32 [2048, 2048], P('seq', 'mp')
- lin_output_grad: float32 [2048, 2048], P('mp', 'seq')
- gain_two_grad: float32 [2048], P('seq')
- win_query_grad: float32 [2048, 2048], P('seq', 'mp')
- win_key_grad: float32 [2048, 2048], P('seq', 'mp')
- win_value_grad: float32 [2048, 2048], P('seq', 'mp')
- win_output_grad: float32 [2048, 2048], P('mp', 'seq')
- gain_three_grad: float32 [2048], P('seq')
- mlp_gate_grad: float32 [2048, 5632], P('seq', 'mp')
- mlp_up_grad: float32 [2048, 5632], P('seq', 'mp')
- mlp_down_grad: float32 [5632, 2048], P('mp', 'seq')
Inputs may be any that keep to these rules, and one draw needn't show every extreme that they name: `group_ids`: never falling, starting at 0 and rising by at most one from a token to the next; one group begins among the first 512 tokens and ends among the last 512 tokens; every draw reaches the largest value.
All inputs are finite; a program needn't handle non-finite values.
Results may differ from a plain program's by a relative error of at most 0.035.
Values may be sent and summed in bfloat16 or wider, within the bound.
A program may use at most 192 MiB of HBM per device.

v0:
```python
import jax
import jax.numpy as jnp
from jax import lax
from jax.sharding import PartitionSpec as P

HD = 128
FEAT = 16
WIN = 64


EPSILON = 1e-05
PRECISE = lax.Precision.HIGHEST


def entering(shard, axis, combine, identity, reverse):
    size, here = (lax.axis_size(axis), lax.axis_index(axis))
    everything = jax.tree.map(
        lambda part, kind: lax.all_gather(part.astype(kind), axis),
        shard,
        (jnp.bfloat16, jnp.bfloat16, jnp.bfloat16),
    )
    start = jax.tree.map(
        lambda part, zero: jnp.broadcast_to(jnp.asarray(zero, part.dtype), part.shape),
        shard,
        identity,
    )

    def turn(k, before):
        at = size - 1 - k if reverse else k
        reached = at > here if reverse else at < here
        new = combine(
            before, jax.tree.map(lambda part, own: part[at].astype(own.dtype), everything, shard)
        )
        return jax.tree.map(lambda a, b: jnp.where(reached, a, b), new, before)

    return lax.fori_loop(0, size, turn, start)


def shifted(shard, axis, by):
    size = lax.axis_size(axis)
    pairs = [(i, i + by) for i in range(size) if 0 <= i + by < size]
    return lax.ppermute(shard, axis, pairs)


def normalize(values, gain_vec):
    factor = lax.rsqrt(jnp.mean(values * values, axis=-1, keepdims=True) + EPSILON)
    return values * factor * gain_vec


def features(values):
    lead_shape = values.shape[:-1]
    feat_width = values.shape[-1]
    outer_prod = (values[..., :, None] * values[..., None, :]).reshape(
        lead_shape + (feat_width * feat_width,)
    )
    return jnp.concatenate(
        [
            jnp.ones(lead_shape + (1,), values.dtype),
            values * feat_width ** (-0.25),
            outer_prod * (2.0 * feat_width) ** (-0.5),
        ],
        axis=-1,
    )


def join_pair(earlier, later):
    early_state, early_norm, early_key = earlier
    late_state, late_norm, late_key = later
    same_key = ((early_key == late_key) | (late_key < 0.0)).astype(jnp.float32)
    return (
        late_state + same_key[..., None, None] * early_state,
        late_norm + same_key[..., None] * early_norm,
        jnp.where(late_key < 0.0, early_key, late_key),
    )


def forward_sum(partial_sum):
    return lax.psum(partial_sum.astype(jnp.bfloat16), "mp").astype(jnp.float32)


def backward_sum(partial_sum):
    return lax.psum(partial_sum.astype(jnp.bfloat16), "mp").astype(jnp.float32)


def weight_grad(left_rows, right_rows):
    return jnp.einsum("ta,tb->ab", left_rows, right_rows, preferred_element_type=jnp.float32)


def input_grad(right_rows, weight_mat):
    return jnp.einsum("tb,ab->ta", right_rows, weight_mat, preferred_element_type=jnp.float32)


def local(
    tokens,
    group_ids,
    gain_one,
    lin_query,
    lin_key,
    lin_value,
    lin_output,
    gain_two,
    win_query,
    win_key,
    win_value,
    win_output,
    gain_three,
    mlp_gate,
    mlp_up,
    mlp_down,
    out_grad,
):
    row_count = tokens.shape[0]
    heads_lin = lin_query.shape[1] // FEAT
    heads_win = win_query.shape[1] // HD
    inputs = tokens.astype(jnp.float32)
    group_float = group_ids.astype(jnp.float32)
    first_key = group_float[0:1]
    last_key = group_float[row_count - 1 :]
    positions = jnp.arange(row_count)
    causal_mask = (
        (positions[None, :] <= positions[:, None]) & (group_ids[None, :] == group_ids[:, None])
    ).astype(jnp.float32)
    last_group = (group_ids == group_ids[row_count - 1]).astype(jnp.float32)
    normed_one = normalize(inputs, gain_one).astype(jnp.bfloat16)
    query_lin = jnp.dot(normed_one, lin_query, preferred_element_type=jnp.float32).reshape(
        row_count, heads_lin, FEAT
    )
    key_lin = jnp.dot(normed_one, lin_key, preferred_element_type=jnp.float32).reshape(
        row_count, heads_lin, FEAT
    )
    value_lin = (
        jnp.dot(normed_one, lin_value, preferred_element_type=jnp.float32)
        .astype(jnp.bfloat16)
        .reshape(row_count, heads_lin, HD)
    )
    query_feat = features(query_lin).astype(jnp.bfloat16)
    key_feat = features(key_lin).astype(jnp.bfloat16)
    query_full = query_feat.astype(jnp.float32)
    key_full = key_feat.astype(jnp.float32)
    value_full = value_lin.astype(jnp.float32)
    kernel_low = (
        jnp.einsum("ihf,jhf->hij", query_feat, key_feat, preferred_element_type=jnp.float32)
        * causal_mask[None]
    ).astype(jnp.bfloat16)
    local_state = jnp.einsum(
        "jhf,jhd->hfd",
        key_feat * last_group.astype(jnp.bfloat16)[:, None, None],
        value_lin,
        preferred_element_type=jnp.float32,
    )
    local_norm = jnp.sum(key_full * last_group[:, None, None], axis=0)
    empty_state = jnp.zeros_like(local_state)
    empty_norm = jnp.zeros_like(local_norm)
    no_key = -jnp.ones((1,), jnp.float32)
    carried_state, carried_norm, prev_key = entering(
        (local_state, local_norm, last_key),
        "seq",
        join_pair,
        (empty_state, empty_norm, no_key),
        False,
    )
    incoming = (group_float == prev_key[0]).astype(jnp.float32)
    numerator = jnp.einsum(
        "hij,jhd->ihd", kernel_low, value_lin, preferred_element_type=jnp.float32
    ) + incoming[:, None, None] * jnp.einsum(
        "ihf,hfd->ihd", query_full, carried_state, precision=PRECISE
    )
    denominator = jnp.transpose(jnp.sum(kernel_low.astype(jnp.float32), axis=2)) + incoming[
        :, None
    ] * jnp.einsum("ihf,hf->ih", query_full, carried_norm, precision=PRECISE)
    quotient = numerator / denominator[:, :, None]
    mixed_lin = quotient.astype(jnp.bfloat16).reshape(row_count, heads_lin * HD)
    resid_one = inputs + forward_sum(
        jnp.dot(mixed_lin, lin_output, preferred_element_type=jnp.float32)
    )
    normed_two = normalize(resid_one, gain_two).astype(jnp.bfloat16)
    query_win = (
        jnp.dot(normed_two, win_query, preferred_element_type=jnp.float32)
        .astype(jnp.bfloat16)
        .reshape(row_count, heads_win, HD)
    )
    key_win = (
        jnp.dot(normed_two, win_key, preferred_element_type=jnp.float32)
        .astype(jnp.bfloat16)
        .reshape(row_count, heads_win, HD)
    )
    value_win = (
        jnp.dot(normed_two, win_value, preferred_element_type=jnp.float32)
        .astype(jnp.bfloat16)
        .reshape(row_count, heads_win, HD)
    )
    tail_flag = last_group[row_count - WIN :].astype(jnp.bfloat16)
    halo_key, halo_value, halo_flag = shifted(
        (key_win[row_count - WIN :], value_win[row_count - WIN :], tail_flag), "seq", 1
    )
    keys_all = jnp.concatenate([halo_key, key_win], axis=0)
    values_all = jnp.concatenate([halo_value, value_win], axis=0)
    key_groups = jnp.concatenate(
        [jnp.where(halo_flag.astype(jnp.float32) > 0.5, prev_key[0], -2.0), group_float]
    )
    key_place = jnp.arange(row_count + WIN) - WIN
    window_mask = (
        (key_place[None, :] <= positions[:, None])
        & (positions[:, None] - key_place[None, :] < WIN)
        & (key_groups[None, :] == group_float[:, None])
    )
    score_scale = HD ** (-0.5)
    scores = (
        jnp.einsum("ihd,jhd->hij", query_win, keys_all, preferred_element_type=jnp.float32)
        * score_scale
    )
    scores = jnp.where(window_mask[None], scores, -1e30)
    row_peak = jnp.max(scores, axis=2, keepdims=True)
    exp_scores = jnp.exp(scores - row_peak)
    attn_probs = exp_scores / jnp.sum(exp_scores, axis=2, keepdims=True)
    probs_low = attn_probs.astype(jnp.bfloat16)
    mixed_win = (
        jnp.einsum("hij,jhd->ihd", probs_low, values_all, preferred_element_type=jnp.float32)
        .astype(jnp.bfloat16)
        .reshape(row_count, heads_win * HD)
    )
    resid_two = resid_one + forward_sum(
        jnp.dot(mixed_win, win_output, preferred_element_type=jnp.float32)
    )
    normed_three = normalize(resid_two, gain_three).astype(jnp.bfloat16)
    gate_act = jnp.dot(normed_three, mlp_gate, preferred_element_type=jnp.float32)
    up_act = jnp.dot(normed_three, mlp_up, preferred_element_type=jnp.float32)
    hidden = (jax.nn.silu(gate_act) * up_act).astype(jnp.bfloat16)
    result = (
        resid_two + forward_sum(jnp.dot(hidden, mlp_down, preferred_element_type=jnp.float32))
    ).astype(jnp.bfloat16)
    down_grad = weight_grad(hidden, out_grad)
    hidden_grad = input_grad(out_grad, mlp_down)
    act_value, act_back = jax.vjp(
        lambda gate_in, up_in: jax.nn.silu(gate_in) * up_in, gate_act, up_act
    )
    gate_grad, up_grad = act_back(hidden_grad)
    gate_low = gate_grad.astype(jnp.bfloat16)
    up_low = up_grad.astype(jnp.bfloat16)
    gate_wgrad = weight_grad(normed_three, gate_low)
    up_wgrad = weight_grad(normed_three, up_low)
    normed_grad = backward_sum(input_grad(gate_low, mlp_gate) + input_grad(up_low, mlp_up))
    norm_value, norm_back = jax.vjp(normalize, resid_two, gain_three)
    resid_grad, gain_three_grad = norm_back(normed_grad)
    grad_two = out_grad.astype(jnp.float32) + resid_grad
    win_low = grad_two.astype(jnp.bfloat16)
    win_output_grad = weight_grad(mixed_win, win_low)
    mixed_grad = (
        input_grad(win_low, win_output).astype(jnp.bfloat16).reshape(row_count, heads_win, HD)
    )
    probs_grad = jnp.einsum(
        "ihd,jhd->hij", mixed_grad, values_all, preferred_element_type=jnp.float32
    )
    values_grad = jnp.einsum(
        "hij,ihd->jhd", probs_low, mixed_grad, preferred_element_type=jnp.float32
    )
    score_grad = attn_probs * (probs_grad - jnp.sum(probs_grad * attn_probs, axis=2, keepdims=True))
    score_low = score_grad.astype(jnp.bfloat16)
    query_grad = (
        jnp.einsum("hij,jhd->ihd", score_low, keys_all, preferred_element_type=jnp.float32)
        * score_scale
    )
    keys_grad = (
        jnp.einsum("hij,ihd->jhd", score_low, query_win, preferred_element_type=jnp.float32)
        * score_scale
    )
    back_key, back_value = (
        shifted(keys_grad[:WIN].astype(jnp.bfloat16), "seq", -1).astype(jnp.float32),
        shifted(values_grad[:WIN].astype(jnp.bfloat16), "seq", -1).astype(jnp.float32),
    )
    key_own = keys_grad[WIN:].at[row_count - WIN :].add(back_key)
    value_own = values_grad[WIN:].at[row_count - WIN :].add(back_value)
    query_win_low = query_grad.astype(jnp.bfloat16).reshape(row_count, heads_win * HD)
    key_win_low = key_own.astype(jnp.bfloat16).reshape(row_count, heads_win * HD)
    value_win_low = value_own.astype(jnp.bfloat16).reshape(row_count, heads_win * HD)
    win_query_grad = weight_grad(normed_two, query_win_low)
    win_key_grad = weight_grad(normed_two, key_win_low)
    win_value_grad = weight_grad(normed_two, value_win_low)
    normed_grad_two = backward_sum(
        input_grad(query_win_low, win_query)
        + input_grad(key_win_low, win_key)
        + input_grad(value_win_low, win_value)
    )
    norm_value_two, norm_back_two = jax.vjp(normalize, resid_one, gain_two)
    resid_grad_two, gain_two_grad = norm_back_two(normed_grad_two)
    grad_one = grad_two + resid_grad_two
    lin_low = grad_one.astype(jnp.bfloat16)
    lin_output_grad = weight_grad(mixed_lin, lin_low)
    mix_grad = (
        lax.optimization_barrier(input_grad(lin_low, lin_output).astype(jnp.bfloat16))
        .astype(jnp.float32)
        .reshape(row_count, heads_lin, HD)
    )
    numer_low = (mix_grad / denominator[:, :, None]).astype(jnp.bfloat16)
    numer_grad = numer_low.astype(jnp.float32)
    denom_grad = -jnp.sum(mix_grad * quotient, axis=2) / denominator
    kernel_grad = (
        (
            jnp.einsum("ihd,jhd->hij", numer_low, value_lin, preferred_element_type=jnp.float32)
            + jnp.transpose(denom_grad)[:, :, None]
        )
        * causal_mask[None]
    ).astype(jnp.bfloat16)
    value_sum = jnp.einsum(
        "hij,ihd->jhd", kernel_low, numer_low, preferred_element_type=jnp.float32
    )
    query_feat_grad = jnp.einsum(
        "hij,jhf->ihf", kernel_grad, key_feat, preferred_element_type=jnp.float32
    ) + incoming[:, None, None] * (
        jnp.einsum("ihd,hfd->ihf", numer_grad, carried_state, precision=PRECISE)
        + denom_grad[:, :, None] * carried_norm[None]
    )
    key_feat_grad = jnp.einsum(
        "hij,ihf->jhf", kernel_grad, query_feat, preferred_element_type=jnp.float32
    )
    query_used = query_full * incoming[:, None, None]
    state_in_grad = jnp.einsum("ihf,ihd->hfd", query_used, numer_grad, precision=PRECISE)
    norm_in_grad = jnp.einsum("ihf,ih->hf", query_used, denom_grad, precision=PRECISE)
    later_state, later_norm, later_key = entering(
        (state_in_grad, norm_in_grad, first_key),
        "seq",
        join_pair,
        (empty_state, empty_norm, no_key),
        True,
    )
    owned_mask = (later_key == last_key).astype(jnp.float32)[0]
    summary_state = owned_mask * later_state
    summary_norm = owned_mask * later_norm
    key_feat_grad = key_feat_grad + last_group[:, None, None] * (
        jnp.einsum("jhd,hfd->jhf", value_full, summary_state, precision=PRECISE)
        + summary_norm[None]
    )
    value_sum = value_sum + last_group[:, None, None] * jnp.einsum(
        "jhf,hfd->jhd", key_full, summary_state, precision=PRECISE
    )
    feat_value, query_back = jax.vjp(features, query_lin)
    feat_value_two, key_back = jax.vjp(features, key_lin)
    query_low = (
        query_back(query_feat_grad)[0].astype(jnp.bfloat16).reshape(row_count, heads_lin * FEAT)
    )
    key_low = key_back(key_feat_grad)[0].astype(jnp.bfloat16).reshape(row_count, heads_lin * FEAT)
    value_low = value_sum.astype(jnp.bfloat16).reshape(row_count, heads_lin * HD)
    lin_query_grad = weight_grad(normed_one, query_low)
    lin_key_grad = weight_grad(normed_one, key_low)
    lin_value_grad = weight_grad(normed_one, value_low)
    normed_grad_one = backward_sum(
        input_grad(query_low, lin_query)
        + input_grad(key_low, lin_key)
        + input_grad(value_low, lin_value)
    )
    norm_value_one, norm_back_one = jax.vjp(normalize, inputs, gain_one)
    resid_grad_one, gain_one_grad = norm_back_one(normed_grad_one)
    tokens_grad = grad_one + resid_grad_one
    reduced = tuple(
        (
            lax.psum_scatter(
                gain_one_grad.astype(jnp.bfloat16), "seq", scatter_dimension=0, tiled=True
            ).astype(jnp.float32),
            lax.psum_scatter(
                lin_query_grad.astype(jnp.bfloat16), "seq", scatter_dimension=0, tiled=True
            ).astype(jnp.float32),
            lax.psum_scatter(
                lin_key_grad.astype(jnp.bfloat16), "seq", scatter_dimension=0, tiled=True
            ).astype(jnp.float32),
            lax.psum_scatter(
                lin_value_grad.astype(jnp.bfloat16), "seq", scatter_dimension=0, tiled=True
            ).astype(jnp.float32),
            lax.psum_scatter(
                lin_output_grad.astype(jnp.bfloat16), "seq", scatter_dimension=1, tiled=True
            ).astype(jnp.float32),
            lax.psum_scatter(
                gain_two_grad.astype(jnp.bfloat16), "seq", scatter_dimension=0, tiled=True
            ).astype(jnp.float32),
            lax.psum_scatter(
                win_query_grad.astype(jnp.bfloat16), "seq", scatter_dimension=0, tiled=True
            ).astype(jnp.float32),
            lax.psum_scatter(
                win_key_grad.astype(jnp.bfloat16), "seq", scatter_dimension=0, tiled=True
            ).astype(jnp.float32),
            lax.psum_scatter(
                win_value_grad.astype(jnp.bfloat16), "seq", scatter_dimension=0, tiled=True
            ).astype(jnp.float32),
            lax.psum_scatter(
                win_output_grad.astype(jnp.bfloat16), "seq", scatter_dimension=1, tiled=True
            ).astype(jnp.float32),
            lax.psum_scatter(
                gain_three_grad.astype(jnp.bfloat16), "seq", scatter_dimension=0, tiled=True
            ).astype(jnp.float32),
            lax.psum_scatter(
                gate_wgrad.astype(jnp.bfloat16), "seq", scatter_dimension=0, tiled=True
            ).astype(jnp.float32),
            lax.psum_scatter(
                up_wgrad.astype(jnp.bfloat16), "seq", scatter_dimension=0, tiled=True
            ).astype(jnp.float32),
            lax.psum_scatter(
                down_grad.astype(jnp.bfloat16), "seq", scatter_dimension=1, tiled=True
            ).astype(jnp.float32),
        )
    )
    return (result, tokens_grad) + reduced


def solution(mesh):
    return jax.shard_map(
        local,
        mesh=mesh,
        in_specs=(
            P("seq", None),
            P("seq"),
            P(),
            P(None, "mp"),
            P(None, "mp"),
            P(None, "mp"),
            P("mp", None),
            P(),
            P(None, "mp"),
            P(None, "mp"),
            P(None, "mp"),
            P("mp", None),
            P(),
            P(None, "mp"),
            P(None, "mp"),
            P("mp", None),
            P("seq", None),
        ),
        out_specs=(
            P("seq", None),
            P("seq", None),
            P("seq"),
            P("seq", "mp"),
            P("seq", "mp"),
            P("seq", "mp"),
            P("mp", "seq"),
            P("seq"),
            P("seq", "mp"),
            P("seq", "mp"),
            P("seq", "mp"),
            P("mp", "seq"),
            P("seq"),
            P("seq", "mp"),
            P("seq", "mp"),
            P("mp", "seq"),
        ),
        check_vma=False,
    )
```

profile of v0, /device:TPU:0, one launch (start us, length us, event | category | flops | bytes accessed | tf_op | source)
XLA Modules:
  0.0 1501.5 jit_solution(6978821488148671930)
XLA Ops:
  8.7 2.1 fusion.20
  22.5 43.0 %all-reduce.6 = (bf16[16]{0:T(256)(128)(2,1)S(1)}, bf16[16]{0:T(256)(128)(2,1)}) all-reduce(bf16[16]{0:T(256)(128)(2,1)S(1)} %dynamic-update-slice.6, bf16[16]{0:T(256)(128)(2,1)S(1)} %dynamic-update-slice.7), channel_id=3, replica_groups=mesh['seq'=16,'mp'=8] {'seq'}, use_global_device_ids=true, to_apply=%add | all-reduce | flops 32 | bytes 128
  66.9 20.4 %all-gather.6 = bf16[16,2,273]{2,1,0:T(2,128)(2,1)S(1)} all-gather(bf16[1,2,273]{2,1,0:T(2,128)(2,1)S(1)} %bitcast.296), channel_id=4, replica_groups=mesh['seq'=16,'mp'=8] {'seq'}, dimensions={0}, use_global_device_ids=true | all-gather | bytes 18564 | tf_op jit(solution)/shard_map/all_gather | solution.py:18
  87.2 2.3 multiply_convert_fusion.10
  92.9 58.7 %while.40 = (s32[]{:T(128)}, f32[2,273,128]{2,1,0:T(8,128)S(1)}, f32[2,273]{1,0:T(2,128)S(1)}, f32[1]{0:T(128)}, s32[]{:T(128)}, /*index=5*/bf16[16,2,273,128]{3...) while((s32[]{:T(128)}, f32[2,273,128]{2,1,0:T(8,128)S(1)}, ...), condition=%wide.region_3.4_spmd.clone, body=%wide.region_2.3_spmd.clone.sunk | while | flops 352180 | bytes 704557 | solution.py:36
  156.5 2.1 convolution_convert_fusion.4
  159.3 3.9 collective-permute-start.1
  165.7 58.4 %all-reduce.14.cloned.1.call-done = bf16[512,2048]{1,0:T(8,128)(2,1)} async-done(((bf16[512,2048]{1,0:T(8,128)(2,1)}), bf16[512,2048]{1,0:T(8,128)(2,1)}) %all-reduce.14.cloned.1.call-update) | async-done | bytes 2097168 | tf_op jit(solution)/shard_map/psum | solution.py:78
  224.1 3.1 multiply_reduce_fusion.1
  230.4 3.7 collective-permute-start.2
  234.8 3.4 collective-permute-start
  241.3 4.2 fusion.82
  245.5 2.6 convolution_convert_fusion.16
  248.0 3.4 convolution_convert_fusion.3
  251.5 65.1 %all-reduce.16.cloned.1.call-done = bf16[512,2048]{1,0:T(8,128)(2,1)} async-done(((bf16[512,2048]{1,0:T(8,128)(2,1)}), bf16[512,2048]{1,0:T(8,128)(2,1)}) %all-reduce.16.cloned.1.call-update) | async-done | bytes 2097168 | tf_op jit(solution)/shard_map/psum | solution.py:78
  316.6 3.9 multiply_reduce_fusion
  328.1 3.2 multiply_convert_fusion.5
  333.2 3.4 add_convert_fusion.2
  337.0 64.8 %all-reduce.18.cloned.1.call-done = bf16[512,2048]{1,0:T(8,128)(2,1)} async-done(((bf16[512,2048]{1,0:T(8,128)(2,1)}), bf16[512,2048]{1,0:T(8,128)(2,1)}) %all-reduce.18.cloned.1.call-update) | async-done | bytes 2097168 | tf_op jit(solution)/shard_map/psum | solution.py:82
  401.9 4.9 fusion.14
  406.8 3.0 fusion.17
  409.8 2.0 convolution_convert_fusion.15
  411.9 3.3 convolution_bitcast_fusion.2
  415.2 2.4 multiply_reduce_fusion.2
  423.7 2.8 fusion.86
  432.9 2.1 fusion.87
  435.8 2.1 add_convert_fusion.1
  438.2 67.6 %all-reduce.20.cloned.1.call-done = bf16[512,2048]{1,0:T(8,128)(2,1)} async-done(((bf16[512,2048]{1,0:T(8,128)(2,1)}), bf16[512,2048]{1,0:T(8,128)(2,1)}) %all-reduce.20.cloned.1.call-update) | async-done | bytes 2097168 | tf_op jit(solution)/shard_map/psum | solution.py:82
  505.8 5.4 fusion.15
  511.2 3.7 fusion.18
  519.7 2.6 convolution_convert_fusion.22
  531.4 4.0 convolution_convert_fusion.6
  535.4 2.3 copy.122
  537.8 3.3 convolution_convert_fusion.9
  541.2 3.3 convolution_convert_fusion.7
  544.6 3.4 convolution_convert_fusion.8
  548.3 3.9 convolution_convert_fusion.10
  552.2 2.3 copy.120
  554.6 5.0 convolution_convert_fusion.2
  559.6 4.6 copy.128
  564.3 5.1 convolution_convert_fusion
  569.4 4.6 copy.126
  575.4 5.0 convolution_convert_fusion.1
  580.4 4.6 copy.124
  585.0 4.3 convolution_convert_fusion.5
  589.4 3.7 fusion.88
  594.5 25.4 %all-gather.7 = bf16[16,2,273]{2,1,0:T(2,128)(2,1)} all-gather(bf16[1,2,273]{2,1,0:T(2,128)(2,1)S(1)} %bitcast.297), channel_id=7, replica_groups=mesh['seq'=16,'mp'=8] {'seq'}, dimensions={0}, use_global_device_ids=true | all-gather | bytes 18564 | tf_op jit(solution)/shard_map/all_gather | solution.py:18
  619.9 78.7 %while.41 = (s32[]{:T(128)}, f32[2,273,128]{2,1,0:T(8,128)S(1)}, f32[2,273]{1,0:T(2,128)S(1)}, f32[1]{0:T(128)}, s32[]{:T(128)}, /*index=5*/bf16[16,2,273,128]{3...) while((s32[]{:T(128)}, f32[2,273,128]{2,1,0:T(8,128)S(1)}, ...), condition=%wide.region_21.22_spmd.clone, body=%wide.region_20.21_spmd.clone.sunk | while | flops 352184 | bytes 704619 | solution.py:36
  707.3 2.0 convolution_multiply_fusion.2
  709.8 2.8 fusion.89
  712.7 5.6 add_convert_fusion
  718.3 3.3 convolution_convert_fusion.11
  725.5 68.8 %reduce-scatter.28.cloned.1.call-done = bf16[128,256]{1,0:T(8,128)(2,1)} async-done(((bf16[2048,256]{1,0:T(8,128)(2,1)}), bf16[128,256]{1,0:T(8,128)(2,1)}) %reduce-scatter.28.cloned.1.call-update) | async-done | bytes 65552 | tf_op jit(solution)/shard_map/reduce_scatter | solution.py:374
  795.7 74.1 %reduce-scatter.32.cloned.1.call-done = bf16[128,256]{1,0:T(8,128)(2,1)} async-done(((bf16[2048,256]{1,0:T(8,128)(2,1)}), bf16[128,256]{1,0:T(8,128)(2,1)}) %reduce-scatter.32.cloned.1.call-update) | async-done | bytes 65552 | tf_op jit(solution)/shard_map/reduce_scatter | solution.py:380
  871.3 74.0 %reduce-scatter.30.cloned.1.call-done = bf16[128,256]{1,0:T(8,128)(2,1)} async-done(((bf16[2048,256]{1,0:T(8,128)(2,1)}), bf16[128,256]{1,0:T(8,128)(2,1)}) %reduce-scatter.30.cloned.1.call-update) | async-done | bytes 65552 | tf_op jit(solution)/shard_map/reduce_scatter | solution.py:377
  946.8 74.2 %reduce-scatter.38.cloned.1.call-done = bf16[128,256]{1,0:T(8,128)(2,1)} async-done(((bf16[2048,256]{1,0:T(8,128)(2,1)}), bf16[128,256]{1,0:T(8,128)(2,1)}) %reduce-scatter.38.cloned.1.call-update) | async-done | bytes 65552
  1022.6 76.9 %reduce-scatter.46.cloned.1.call-done = bf16[128,704]{1,0:T(8,128)(2,1)} async-done(((bf16[2048,704]{1,0:T(8,128)(2,1)}), bf16[128,704]{1,0:T(8,128)(2,1)}) %reduce-scatter.46.cloned.1.call-update) | async-done | bytes 180240
  1101.3 76.4 %reduce-scatter.44.cloned.1.call-done = bf16[128,704]{1,0:T(8,128)(2,1)} async-done(((bf16[2048,704]{1,0:T(8,128)(2,1)}), bf16[128,704]{1,0:T(8,128)(2,1)}) %reduce-scatter.44.cloned.1.call-update) | async-done | bytes 180240
  1179.5 76.5 %reduce-scatter.42.cloned.1.call-done = bf16[128,704]{1,0:T(8,128)(2,1)} async-done(((bf16[2048,704]{1,0:T(8,128)(2,1)}), bf16[128,704]{1,0:T(8,128)(2,1)}) %reduce-scatter.42.cloned.1.call-update) | async-done | bytes 180240
  1257.9 72.8 %reduce-scatter.36.cloned.1.call-done = bf16[128,32]{1,0:T(8,128)(2,1)} async-done(((bf16[2048,32]{1,0:T(8,128)(2,1)}), bf16[128,32]{1,0:T(8,128)(2,1)}) %reduce-scatter.36.cloned.1.call-update) | async-done | bytes 8208
  1332.1 72.7 %all-reduce.22.cloned.1.call-done = (bf16[512,2048]{1,0:T(8,128)(2,1)}, bf16[512,2048]{1,0:T(8,128)(2,1)}) async-done(((bf16[512,2048]{1,0:T(8,128)(2,1)}, bf16[512,2048]{1,0:T(8,128)(2,1)}), (bf16[512,2048]{1,0:T(8,128)(2,1)}, bf16[512,2048]{1,0:T(8,128)(2,1)})) %all-reduce.22.cloned.1.call-update) | async-done | bytes 4194320 | tf_op jit(solution)/shard_map/psum | solution.py:78
  1404.8 4.0 fusion.16
  1408.8 74.6 %all-reduce.5 = (bf16[2048]{0:T(1024)(128)(2,1)S(1)}, bf16[2048]{0:T(1024)(128)(2,1)S(1)}, bf16[2048]{0:T(1024)(128)(2,1)S(1)}) all-reduce(bf16[2048]{0:T(1024)(128)(2,1)S(1)} %get-tuple-element.445, bf16[2048]{0:T(1024)(128)(2,1)S(1)} %copy-done.88, bf16[2048]{0:T(1024)(128)(2,1)S(1)} %copy-done.87), channel_id=8, replica_groups=mesh['seq'=16,'mp'=8] {'seq'}, use_global_device_ids=true, to_apply=%region_27.28.clone | all-reduce | flops 6144 | bytes 24576
  1484.6 8.1 fusion.19
  (451 shorter events, 174.0 us)
Async XLA Ops:
  7.2 320.9 %copy-start = (bf16[704,2048]{1,0:T(8,128)(2,1)S(1)}, bf16[704,2048]{1,0:T(8,128)(2,1)}, u32[]{:S(2)}) copy-start(bf16[704,2048]{1,0:T(8,128)(2,1)} %param.40) | copy-start | bytes 8650756
  7.2 4.2 copy-start.68
  7.2 4.9 copy-start.67
  7.2 85.7 %all-gather.11.cloned.1.call-start = ((), (), s32[]{:S(2)}) async-start(), calls=%async_computation.19 | async-start | bytes 2437120 | tf_op jit(solution)/shard_map/all_gather | solution.py:18
  7.3 4.8 copy-start.1
  12.1 3.9 copy-start.94
  12.1 53.4 %copy-start.73 = (f32[512]{0:T(512)}, f32[512]{0:T(512)S(1)}, u32[]{:S(2)}) copy-start(f32[512]{0:T(512)S(1)} %get-tuple-element.493) | copy-start | bytes 6148
  15.8 71.5 %copy-start.56 = (bf16[2048,32]{0,1:T(8,128)(2,1)S(1)}, bf16[2048,32]{0,1:T(8,128)(2,1)}, u32[]{:S(2)}) copy-start(bf16[2048,32]{0,1:T(8,128)(2,1)} %param.28) | copy-start | bytes 393220
  15.9 137.4 %copy-start.84 = (bf16[273]{0:T(512)(128)(2,1)}, bf16[273]{0:T(512)(128)(2,1)S(1)}, u32[]{:S(2)}) copy-start(bf16[273]{0:T(512)(128)(2,1)S(1)} %pad.9.clone) | copy-start | bytes 1642
  17.9 206.2 %all-reduce.14.cloned.1.call-start = ((), (), s32[]{:S(2)}) async-start(), calls=%async_computation.11 | async-start | bytes 4194304 | tf_op jit(solution)/shard_map/psum | solution.py:78
  17.9 4.6 copy-start.81
  66.8 24.1 %copy-start.18 = (bf16[512,2,16,16]{0,3,2,1:T(8,128)(2,1)S(1)}, bf16[512,2,16,16]{0,3,2,1:T(8,128)(2,1)}, u32[]{:S(2)}) copy-start(bf16[512,2,16,16]{0,3,2,1:T(8,128)(2,1)} %copy-done.17) | copy-start | bytes 1572868
  89.6 63.8 %copy-start.63 = (bf16[512,2,16]{0,2,1:T(8,128)(2,1)}, bf16[512,2,16]{0,2,1:T(8,128)(2,1)S(1)}, u32[]{:S(2)}) copy-start(bf16[512,2,16]{0,2,1:T(8,128)(2,1)S(1)} %get-tuple-element.503) | copy-start | bytes 98308
  151.7 4.8 copy-start.77
  158.5 6.0 copy-start.82
  158.6 6.0 copy-start.83
  158.6 158.0 %all-reduce.16.cloned.1.call-start = ((), (), s32[]{:S(2)}) async-start(), calls=%async_computation.12 | async-start | bytes 4194304 | tf_op jit(solution)/shard_map/psum | solution.py:78
  159.3 5.2 collective-permute-start.1
  164.6 63.8 %copy-start.66 = (f32[2048]{0:T(1024)S(1)}, f32[2048]{0:T(1024)}, u32[]{:S(2)}) copy-start(f32[2048]{0:T(1024)} %param.32) | copy-start | bytes 24580
  224.1 4.3 copy-start.2
  224.1 4.3 copy-start.12
  229.6 8.6 copy-start.29
  229.6 4.5 copy-start.42
  230.3 7.9 copy-start.50
  230.4 9.5 collective-permute-start.2
  234.8 5.0 collective-permute-start
  251.4 69.1 %copy-start.65 = (f32[2048]{0:T(1024)S(1)}, f32[2048]{0:T(1024)}, u32[]{:S(2)}) copy-start(f32[2048]{0:T(1024)} %param.37) | copy-start | bytes 24580
  251.5 150.4 %all-reduce.18.cloned.1.call-start = ((), (), s32[]{:S(2)}) async-start(), calls=%async_computation.13 | async-start | bytes 4194304 | tf_op jit(solution)/shard_map/psum | solution.py:82
  336.6 169.2 %all-reduce.20.cloned.1.call-start = ((), (), s32[]{:S(2)}) async-start(), calls=%async_computation.14 | async-start | bytes 4194304 | tf_op jit(solution)/shard_map/psum | solution.py:82
  401.9 4.9 copy-start.5
  401.9 4.9 copy-start.16
  418.4 5.3 copy-start.51
  419.9 6.5 copy-start.39
  420.4 6.7 copy-start.41
  420.4 7.5 collective-permute-start.4
  422.4 8.0 collective-permute-start.3
  437.9 67.9 %copy-start.72 = (f32[512]{0:T(512)S(1)}, f32[512]{0:T(512)}, u32[]{:S(2)}) copy-start(f32[512]{0:T(512)} %copy-done.71) | copy-start | bytes 6148
  438.0 73.2 %copy-start.80 = (f32[512]{0:T(512)S(1)}, f32[512]{0:T(512)}, u32[]{:S(2)}) copy-start(f32[512]{0:T(512)} %copy-done.79) | copy-start | bytes 6148
  438.0 181.9 %all-gather.13.cloned.1.call-start = ((), (), s32[]{:S(2)}) async-start(), calls=%async_computation.20 | async-start | bytes 2437120 | tf_op jit(solution)/shard_map/all_gather | solution.py:18
  505.8 5.4 copy-start.3
  505.8 5.4 copy-start.7
  511.2 5.7 copy-start.24
  522.3 200.0 %reduce-scatter.34.cloned.1.call-start = ((), (), s32[]{:S(2)}) async-start(), calls=%async_computation.21 | async-start | bytes 557056
  527.3 4.0 copy-start.37
  531.3 192.5 %reduce-scatter.40.cloned.1.call-start = ((), (), s32[]{:S(2)}) async-start(), calls=%async_computation.24 | async-start | bytes 1114112
  537.7 256.5 %reduce-scatter.28.cloned.1.call-start = ((), (), s32[]{:S(2)}) async-start(), calls=%async_computation.16 | async-start | bytes 1114112 | tf_op jit(solution)/shard_map/reduce_scatter | solution.py:374
  541.1 328.7 %reduce-scatter.32.cloned.1.call-start = ((), (), s32[]{:S(2)}) async-start(), calls=%async_computation.18 | async-start | bytes 1114112 | tf_op jit(solution)/shard_map/reduce_scatter | solution.py:380
  544.5 3.8 copy-start.35
  544.5 400.7 %reduce-scatter.30.cloned.1.call-start = ((), (), s32[]{:S(2)}) async-start(), calls=%async_computation.17 | async-start | bytes 1114112 | tf_op jit(solution)/shard_map/reduce_scatter | solution.py:377
  548.1 472.9 %reduce-scatter.38.cloned.1.call-start = ((), (), s32[]{:S(2)}) async-start(), calls=%async_computation.23 | async-start | bytes 1114112
  554.5 544.9 %reduce-scatter.46.cloned.1.call-start = ((), (), s32[]{:S(2)}) async-start(), calls=%async_computation.27 | async-start | bytes 3342336
  564.3 613.4 %reduce-scatter.44.cloned.1.call-start = ((), (), s32[]{:S(2)}) async-start(), calls=%async_computation.26 | async-start | bytes 3342336
  574.0 682.0 %reduce-scatter.42.cloned.1.call-start = ((), (), s32[]{:S(2)}) async-start(), calls=%async_computation.25 | async-start | bytes 3342336
  589.3 3.8 copy-start.90
  589.3 741.3 %reduce-scatter.36.cloned.1.call-start = ((), (), s32[]{:S(2)}) async-start(), calls=%async_computation.22 | async-start | bytes 557056
  589.4 3.7 copy-start.31
  589.4 3.7 copy-start.64
  594.5 104.9 %copy-start.74 = (f32[512]{0:T(512)S(1)}, f32[512]{0:T(512)}, u32[]{:S(2)}) copy-start(f32[512]{0:T(512)} %copy-done.73) | copy-start | bytes 6148
  712.6 692.2 %all-reduce.22.cloned.1.call-start = ((), (), s32[]{:S(2)}) async-start(), calls=%async_computation.28 | async-start | bytes 8388608 | tf_op jit(solution)/shard_map/psum | solution.py:78
  718.3 774.4 %reduce-scatter.26.cloned.1.call-start = ((), (), s32[]{:S(2)}) async-start(), calls=%async_computation.15 | async-start | bytes 1114112 | tf_op jit(solution)/shard_map/reduce_scatter | solution.py:365
  721.7 683.1 %copy-start.70 = (f32[512]{0:T(512)S(1)}, f32[512]{0:T(512)}, u32[]{:S(2)}) copy-start(f32[512]{0:T(512)} %copy-done.69) | copy-start | bytes 6148
  1404.8 4.0 copy-start.87
  1404.8 4.0 copy-start.88
  1404.8 79.8 %copy-start.76 = (f32[512]{0:T(512)S(1)}, f32[512]{0:T(512)}, u32[]{:S(2)}) copy-start(f32[512]{0:T(512)} %copy-done.75) | copy-start | bytes 6148
  (57 other events, 115.5 us)
Sparse Core Ops, SparseCore 0:
  18.0 48.3 all-gather.10
  158.7 65.3 all-reduce.13
  251.6 65.0 all-reduce.15
  336.7 65.1 all-reduce.17
  438.1 67.6 all-reduce.19
  522.4 45.4 all-gather.12
  571.1 71.7 reduce-scatter.33
  646.4 72.3 reduce-scatter.39
  722.0 72.1 reduce-scatter.27
  797.6 72.1 reduce-scatter.31
  873.0 72.2 reduce-scatter.29
  948.7 72.2 reduce-scatter.37
  1024.3 75.1 reduce-scatter.45
  1102.6 74.9 reduce-scatter.43
  1180.8 75.1 reduce-scatter.41
  1259.1 71.5 reduce-scatter.35
  1333.1 71.6 all-reduce.21
  1408.2 73.2 reduce-scatter.25
where the time goes:
time: 1510 us; the launch traced here: 1500 us
  waiting for transfers between devices  924 us (61%)
  blocking collectives  163 us (11%)
  matrix products  122 us (8%)
  other arithmetic  108 us (7%)
  local copies, waits for them, and re-layouts  87.6 us (6%)
  loops' own time  63.7 us (4%)
  between operations  17.5 us (1%)
  starting transfers between devices  15.1 us (1%)
    unnamed x25, waiting for transfers between devices  377 us
    psum x3, waiting for transfers between devices, forward_sum(): return lax.psum(partial_sum.astype(jnp.bfloat16), 'mp').astype(jnp.float32)  196 us
    psum x2, waiting for transfers between devices, backward_sum(): return lax.psum(partial_sum.astype(jnp.bfloat16), 'mp').astype(jnp.float32)  132 us
    unnamed x2, blocking collectives  118 us
    reduce_scatter x1, waiting for transfers between devices, local(): lax.psum_scatter(win_value_grad.astype(jnp.bfloat16), 'seq', scatter_dime...  74.1 us
    reduce_scatter x1, waiting for transfers between devices, local(): lax.psum_scatter(win_key_grad.astype(jnp.bfloat16), 'seq', scatter_dimens...  74 us
    reduce_scatter x1, waiting for transfers between devices, local(): lax.psum_scatter(win_query_grad.astype(jnp.bfloat16), 'seq', scatter_dime...  68.8 us
    another operation x2, loops' own time, entering(): return lax.fori_loop(0, size, turn, start)  63.7 us
  transfers between devices with their start and end apart: 23, of which 15 were waited for; matrix products, arithmetic and copies ran while one was open for 13% of the time, Pallas kernels for 0%

commit v1 on v0

--- a/solution.py
+++ b/solution.py
@@ -1,39 +1,512 @@
+import functools
+
 import jax
 import jax.numpy as jnp
 from jax import lax
+from jax.experimental import pallas as pl
+from jax.experimental.pallas import tpu as pltpu
 from jax.sharding import PartitionSpec as P
 
 HD = 128
 FEAT = 16
 WIN = 64
-
+D = 2048
+ROWS = 512
+HALF_ROWS = 256
+OWN = 64
+PIECE = 32
 
 EPSILON = 1e-05
 PRECISE = lax.Precision.HIGHEST
-
-
-def entering(shard, axis, combine, identity, reverse):
-    size, here = (lax.axis_size(axis), lax.axis_index(axis))
-    everything = jax.tree.map(
-        lambda part, kind: lax.all_gather(part.astype(kind), axis),
-        shard,
-        (jnp.bfloat16, jnp.bfloat16, jnp.bfloat16),
-    )
-    start = jax.tree.map(
-        lambda part, zero: jnp.broadcast_to(jnp.asarray(zero, part.dtype), part.shape),
-        shard,
-        identity,
-    )
-
-    def turn(k, before):
-        at = size - 1 - k if reverse else k
-        reached = at > here if reverse else at < here
-        new = combine(
-            before, jax.tree.map(lambda part, own: part[at].astype(own.dtype), everything, shard)
+MESH = pl.DeviceIdType.MESH
+BF = jnp.bfloat16
+F32 = jnp.float32
+VMEM_LIMIT = 60 * 1024 * 1024
+
+
+class Place:
+    def __init__(self):
+        self.seq = lax.axis_index("seq")
+        self.mp = lax.axis_index("mp")
+        self.z, self.y = self.seq // 4, self.seq % 4
+        self.x, self.core = self.mp // 2, self.mp % 2
+
+    def peer(self):
+        return (self.seq, self.x * 2 + (1 - self.core))
+
+    def on_x(self, step):
+        return (self.seq, ((self.x + step) % 4) * 2 + self.core)
+
+    def on_y(self, step):
+        return (self.z * 4 + (self.y + step) % 4, self.mp)
+
+    def on_z(self, step):
+        return (((self.z + step) % 4) * 4 + self.y, self.mp)
+
+
+class Copies:
+    def __init__(self, send_sems, recv_sems):
+        self.send_sems, self.recv_sems, self.count, self.started = send_sems, recv_sems, 0, []
+
+    def make(self, src, dst, device):
+        k = self.count
+        self.count += 1
+        return pltpu.make_async_remote_copy(
+            src_ref=src,
+            dst_ref=dst,
+            send_sem=self.send_sems.at[k],
+            recv_sem=self.recv_sems.at[k],
+            device_id=device,
+            device_id_type=MESH,
         )
-        return jax.tree.map(lambda a, b: jnp.where(reached, a, b), new, before)
-
-    return lax.fori_loop(0, size, turn, start)
+
+    def start(self, src, dst, device):
+        copy = self.make(src, dst, device)
+        copy.start()
+        self.started.append(copy)
+        return copy
+
+    def finish(self):
+        for copy in self.started:
+            copy.wait_send()
+
+
+def greet(devices):
+    barrier = pltpu.get_barrier_semaphore()
+    for device in devices:
+        pl.semaphore_signal(barrier, inc=1, device_id=device, device_id_type=MESH)
+    pl.semaphore_wait(barrier, len(devices))
+
+
+def rows_at(start, size):
+    return pl.ds(pl.multiple_of(start, 16), size)
+
+
+def sum_over_mp(place, copies, part, from_peer, send_opp, send_right, send_left, fwd, comb, direct, own):
+    x, core = place.x, place.core
+    peer, right, left = place.peer(), place.on_x(1), place.on_x(3)
+    mine, other = core * HALF_ROWS, (1 - core) * HALF_ROWS
+    order = [(x + 2) % 4, (x + 1) % 4, (x + 3) % 4, x]
+    exchange = [
+        copies.start(
+            part.at[rows_at(other + at * OWN, OWN)], from_peer.at[rows_at(at * OWN, OWN)], peer
+        )
+        for at in order
+    ]
+
+    def chip_sum(at, low, size):
+        return part[rows_at(mine + at * OWN + low, size)].astype(F32) + from_peer[
+            rows_at(at * OWN + low, size)
+        ].astype(F32)
+
+    exchange[0].wait_recv()
+    send_opp[...] = chip_sum(order[0], 0, OWN).astype(BF)
+    to_right = copies.start(send_opp.at[0:PIECE], fwd.at[0], right)
+    to_left = copies.start(send_opp.at[PIECE:OWN], fwd.at[1], left)
+    exchange[1].wait_recv()
+    send_right[0] = chip_sum(order[1], PIECE, PIECE).astype(BF)
+    direct_right = copies.start(send_right.at[0], direct.at[1], right)
+    exchange[2].wait_recv()
+    send_left[0] = chip_sum(order[2], 0, PIECE).astype(BF)
+    direct_left = copies.start(send_left.at[0], direct.at[0], left)
+    to_right.wait_recv()
+    send_right[1] = (chip_sum(order[1], 0, PIECE) + fwd[0].astype(F32)).astype(BF)
+    comb_right = copies.start(send_right.at[1], comb.at[0], right)
+    to_left.wait_recv()
+    send_left[1] = (chip_sum(order[2], PIECE, PIECE) + fwd[1].astype(F32)).astype(BF)
+    comb_left = copies.start(send_left.at[1], comb.at[1], left)
+    exchange[3].wait_recv()
+    own[...] = chip_sum(order[3], 0, OWN)
+    direct_left.wait_recv()
+    own[0:PIECE] += direct[0].astype(F32)
+    direct_right.wait_recv()
+    own[PIECE:OWN] += direct[1].astype(F32)
+    comb_right.wait_recv()
+    own[0:PIECE] += comb[0].astype(F32)
+    comb_left.wait_recv()
+    own[PIECE:OWN] += comb[1].astype(F32)
+
+
+def gather_over_mp(place, copies, full):
+    x, core = place.x, place.core
+    peer, right, left = place.peer(), place.on_x(1), place.on_x(3)
+    base, other = core * HALF_ROWS, (1 - core) * HALF_ROWS
+
+    def block(at, low, size):
+        return full.at[rows_at(base + at * OWN + low, size)]
+
+    def send(at, low, size, device):
+        return copies.start(block(at, low, size), block(at, low, size), device)
+
+    def expect(at, low, size, copy):
+        copy.wait_recv()
+
+    right_at, left_at, opp_at = (x + 1) % 4, (x + 3) % 4, (x + 2) % 4
+    right_low = send(x, 0, PIECE, right)
+    left_high = send(x, PIECE, PIECE, left)
+    right_high = send(x, PIECE, PIECE, right)
+    left_low = send(x, 0, PIECE, left)
+    peers = [send(x, 0, OWN, peer)]
+    right_low.wait_recv()
+    fwd_right = send(left_at, 0, PIECE, right)
+    left_high.wait_recv()
+    fwd_left = send(right_at, PIECE, PIECE, left)
+    right_high.wait_recv()
+    peers.append(send(left_at, 0, OWN, peer))
+    left_low.wait_recv()
+    peers.append(send(right_at, 0, OWN, peer))
+    fwd_right.wait_recv()
+    peers.append(send(opp_at, 0, PIECE, peer))
+    fwd_left.wait_recv()
+    peers.append(send(opp_at, PIECE, PIECE, peer))
+    for copy in peers:
+        copy.wait_recv()
+
+
+MP_COPIES = 4 + 6 + 6 + 5
+
+
+def mp_scratch():
+    return [
+        pltpu.VMEM((HALF_ROWS, D), BF),
+        pltpu.VMEM((OWN, D), BF),
+        pltpu.VMEM((2, PIECE, D), BF),
+        pltpu.VMEM((2, PIECE, D), BF),
+        pltpu.VMEM((2, PIECE, D), BF),
+        pltpu.VMEM((2, PIECE, D), BF),
+        pltpu.VMEM((2, PIECE, D), BF),
+        pltpu.VMEM((OWN, D), F32),
+        pltpu.SemaphoreType.DMA((MP_COPIES,)),
+        pltpu.SemaphoreType.DMA((MP_COPIES,)),
+    ]
+
+
+def own_start(place):
+    return place.core * HALF_ROWS + place.x * OWN
+
+
+def mp_forward_kernel(part, resid, gain, full, resid_out, *scratch):
+    place = Place()
+    *bufs, own, send_sems, recv_sems = scratch
+    copies = Copies(send_sems, recv_sems)
+    greet([place.peer(), place.on_x(1), place.on_x(3)])
+    sum_over_mp(place, copies, part, *bufs, own)
+    rows = own[...] + resid[...]
+    resid_out[...] = rows
+    factor = lax.rsqrt(jnp.mean(rows * rows, axis=-1, keepdims=True) + EPSILON)
+    full[rows_at(own_start(place), OWN)] = (rows * factor * gain[...]).astype(BF)
+    gather_over_mp(place, copies, full)
+    copies.finish()
+
+
+def mp_plain_kernel(part, resid, full, *scratch):
+    place = Place()
+    *bufs, own, send_sems, recv_sems = scratch
+    copies = Copies(send_sems, recv_sems)
+    greet([place.peer(), place.on_x(1), place.on_x(3)])
+    sum_over_mp(place, copies, part, *bufs, own)
+    full[rows_at(own_start(place), OWN)] = (own[...] + resid[...]).astype(BF)
+    gather_over_mp(place, copies, full)
+    copies.finish()
+
+
+def mp_backward_kernel(part, resid, gain, grad, full, grad_out, gain_out, *scratch):
+    place = Place()
+    *bufs, own, send_sems, recv_sems = scratch
+    copies = Copies(send_sems, recv_sems)
+    greet([place.peer(), place.on_x(1), place.on_x(3)])
+    sum_over_mp(place, copies, part, *bufs, own)
+    rows, normed_grad = resid[...], own[...]
+    factor = lax.rsqrt(jnp.mean(rows * rows, axis=-1, keepdims=True) + EPSILON)
+    normed = rows * factor
+    scaled = normed_grad * gain[...]
+    total = grad[...] + factor * (
+        scaled - normed * jnp.mean(scaled * normed, axis=-1, keepdims=True)
+    )
+    grad_out[...] = total
+    gain_out[...] = jnp.sum(normed_grad * normed, axis=0, keepdims=True)
+    full[rows_at(own_start(place), OWN)] = total.astype(BF)
+    gather_over_mp(place, copies, full)
+    copies.finish()
+
+
+def vmem(count):
+    return [pl.BlockSpec(memory_space=pltpu.VMEM)] * count
+
+
+def call(kernel, outs, scratch, collective_id, *args):
+    return pl.pallas_call(
+        kernel,
+        out_shape=outs,
+        in_specs=vmem(len(args)),
+        out_specs=vmem(len(outs)),
+        scratch_shapes=scratch,
+        compiler_params=pltpu.CompilerParams(
+            collective_id=collective_id, has_side_effects=True, vmem_limit_bytes=VMEM_LIMIT
+        ),
+    )(*args)
+
+
+def shape(dims, kind):
+    return jax.ShapeDtypeStruct(dims, kind)
+
+
+def mp_forward(part, resid, gain):
+    return call(
+        mp_forward_kernel,
+        (shape((ROWS, D), BF), shape((OWN, D), F32)),
+        mp_scratch(),
+        0,
+        part.astype(BF),
+        resid,
+        gain.reshape(1, D),
+    )
+
+
+def mp_plain(part, resid):
+    return call(mp_plain_kernel, (shape((ROWS, D), BF),), mp_scratch(), 1, part.astype(BF), resid)[0]
+
+
+def mp_backward(part, resid, gain, grad):
+    return call(
+        mp_backward_kernel,
+        (shape((ROWS, D), BF), shape((OWN, D), F32), shape((1, D), F32)),
+        mp_scratch(),
+        2,
+        part.astype(BF),
+        resid,
+        gain.reshape(1, D),
+        grad,
+    )
+
+
+STATE_ROWS = 576
+STATE_HALF = 288
+
+
+def ring_gather(copies, right, left, held):
+    low, high = pl.ds(0, STATE_HALF), pl.ds(STATE_HALF, STATE_HALF)
+    right_low = copies.start(held.at[0, low], held.at[1, low], right)
+    left_high = copies.start(held.at[0, high], held.at[3, high], left)
+    right_high = copies.start(held.at[0, high], held.at[1, high], right)
+    left_low = copies.start(held.at[0, low], held.at[3, low], left)
+    right_low.wait_recv()
+    fwd_right = copies.start(held.at[1, low], held.at[2, low], right)
+    left_high.wait_recv()
+    fwd_left = copies.start(held.at[3, high], held.at[2, high], left)
+    for copy in (right_high, left_low, fwd_right, fwd_left):
+        copy.wait_recv()
+
+
+def state_kernel(reverse, state, out, held_y, held_z, send_sems, recv_sems):
+    place = Place()
+    copies = Copies(send_sems, recv_sems)
+    right_y, left_y = place.on_y(1), place.on_y(3)
+    right_z, left_z = place.on_z(1), place.on_z(3)
+    greet([right_y, left_y, right_z, left_z])
+    held_y[0] = state[...]
+    ring_gather(copies, right_y, left_y, held_y)
+    parts = [held_y[k].astype(F32) for k in range(4)]
+    held_z[0] = (parts[0] + parts[1] + parts[2] + parts[3]).astype(BF)
+
+    def counted(position, step):
+        at = (position - step + 4) % 4
+        reached = at > position if reverse else at < position
+        return jnp.where(reached, 1.0, 0.0)
+
+    total = jnp.zeros((STATE_ROWS, HD), F32)
+    for step in range(1, 4):
+        total = total + counted(place.y, step) * parts[step]
+    out[...] = total
+    ring_gather(copies, right_z, left_z, held_z)
+    total = out[...]
+    for step in range(1, 4):
+        total = total + counted(place.z, step) * held_z[step].astype(F32)
+    out[...] = total
+    copies.finish()
+
+
+def state_scan(state, norm, reverse):
+    heads, width = norm.shape
+    flat = jnp.concatenate(
+        [
+            state.reshape(heads * width, HD),
+            jnp.pad(norm.reshape(-1), (0, 5 * HD - heads * width)).reshape(5, HD),
+        ]
+    ).astype(BF)
+    flat = jnp.pad(flat, ((0, STATE_ROWS - flat.shape[0]), (0, 0)))
+    out = call(
+        functools.partial(state_kernel, reverse),
+        (shape((STATE_ROWS, HD), F32),),
+        [
+            pltpu.VMEM((4, STATE_ROWS, HD), BF),
+            pltpu.VMEM((4, STATE_ROWS, HD), BF),
+            pltpu.SemaphoreType.DMA((12,)),
+            pltpu.SemaphoreType.DMA((12,)),
+        ],
+        4 if reverse else 3,
+        flat,
+    )[0]
+    count = heads * width
+    return (
+        out[:count].reshape(heads, width, HD),
+        out[count : count + 5].reshape(-1)[:count].reshape(heads, width),
+    )
+
+
+COLS = 3712
+
+
+class Ring:
+    def __init__(self, copies, right, left, pick, bufs):
+        self.copies, self.right, self.left, self.pick = copies, right, left, pick
+        self.fwd, self.direct, self.comb, self.out = bufs
+
+    def first(self):
+        copies, pick = self.copies, self.pick
+        self.fwd_right = copies.start(pick(2, 0), self.fwd.at[0], self.right)
+        self.fwd_left = copies.start(pick(2, 1), self.fwd.at[1], self.left)
+        self.direct_right = copies.start(pick(1, 1), self.direct.at[1], self.right)
+        self.direct_left = copies.start(pick(3, 0), self.direct.at[0], self.left)
+
+    def second(self):
+        self.fwd_right.wait_recv()
+        self.out[0] = (self.pick(1, 0)[...].astype(F32) + self.fwd[0].astype(F32)).astype(BF)
+        self.comb_right = self.copies.start(self.out.at[0], self.comb.at[0], self.right)
+        self.fwd_left.wait_recv()
+        self.out[1] = (self.pick(3, 1)[...].astype(F32) + self.fwd[1].astype(F32)).astype(BF)
+        self.comb_left = self.copies.start(self.out.at[1], self.comb.at[1], self.left)
+
+    def total(self, half):
+        (self.direct_left if half == 0 else self.direct_right).wait_recv()
+        (self.comb_right if half == 0 else self.comb_left).wait_recv()
+        return (
+            self.pick(0, half)[...].astype(F32)
+            + self.direct[half].astype(F32)
+            + self.comb[half].astype(F32)
+        )
+
+
+SPLITS = ((0, 1024), (1024, 1024), (2048, 896), (2944, 768))
+
+
+def seq_kernel(grads, gains, out, gains_out, *scratch):
+    place = Place()
+    send_sems, recv_sems = scratch[-2:]
+    gain_y, gain_z, gain_zz, gain_x, gain_xx, gain_p, gain_pp = scratch[-9:-2]
+    bufs = scratch[:-9]
+    copies = Copies(send_sems, recv_sems)
+    z, y = place.z, place.y
+    ring_y, ring_z = (place.on_y(1), place.on_y(3)), (place.on_z(1), place.on_z(3))
+    greet(
+        [place.on_y(k) for k in (1, 2, 3)]
+        + [place.on_z(k) for k in (1, 2, 3)]
+        + [place.on_x(k) for k in (1, 2, 3)]
+        + [place.peer()]
+    )
+    stages = []
+    for number, (at, width) in enumerate(SPLITS):
+        cols = pl.ds(at, width)
+        mine = bufs[number * 10 : number * 10 + 10]
+
+        def pick_a(k, half, cols=cols):
+            return grads.at[:, (y + k) % 4, pl.ds(half * 32, 32), cols]
+
+        def pick_b(k, half, cols=cols):
+            return grads.at[(z + k) % 4, :, pl.ds(64 + half * 32, 32), cols]
+
+        first_a = Ring(copies, *ring_y, pick_a, mine[0:4])
+        first_b = Ring(copies, *ring_z, pick_b, mine[4:8])
+        sum_a, sum_b = mine[8], mine[9]
+
+        stages.append((number, cols, width, first_a, first_b, sum_a, sum_b))
+    for stage in stages:
+        stage[3].first()
+        stage[4].first()
+    for number, cols, width, first_a, first_b, sum_a, sum_b in stages:
+        first_a.second()
+        first_b.second()
+    second = []
+    offset = len(SPLITS) * 10
+    for number, cols, width, first_a, first_b, sum_a, sum_b in stages:
+        for half in range(2):
+            sum_a[:, half] = first_a.total(half).astype(BF)
+            sum_b[:, half] = first_b.total(half).astype(BF)
+
+        def pick_c(k, half, ref=sum_a):
+            return ref.at[(z + k) % 4, half]
+
+        def pick_d(k, half, ref=sum_b):
+            return ref.at[(y + k) % 4, half]
+
+        extra = bufs[offset + number * 8 : offset + number * 8 + 8]
+        second_a = Ring(copies, *ring_z, pick_c, extra[0:4])
+        second_b = Ring(copies, *ring_y, pick_d, extra[4:8])
+        second_a.first()
+        second_b.first()
+        second.append((cols, second_a, second_b))
+    for cols, second_a, second_b in second:
+        second_a.second()
+        second_b.second()
+    over_y = [
+        copies.start(gains.at[:, (y + k) % 4], gain_y.at[k - 1], place.on_y(k)) for k in (1, 2, 3)
+    ]
+    total = gains[:, pl.ds(y, 1)][:, 0].astype(F32)
+    for k, copy in enumerate(over_y):
+        copy.wait_recv()
+        total = total + gain_y[k].astype(F32)
+    gain_z[...] = total.astype(BF)
+    over_z = [
+        copies.start(gain_z.at[(z + k) % 4], gain_zz.at[k - 1], place.on_z(k)) for k in (1, 2, 3)
+    ]
+    total = gain_z[z].astype(F32)
+    for k, copy in enumerate(over_z):
+        copy.wait_recv()
+        total = total + gain_zz[k].astype(F32)
+    gain_x[...] = total.astype(BF)
+    over_x = [copies.start(gain_x, gain_xx.at[k - 1], place.on_x(k)) for k in (1, 2, 3)]
+    total = gain_x[...].astype(F32)
+    for k, copy in enumerate(over_x):
+        copy.wait_recv()
+        total = total + gain_xx[k].astype(F32)
+    gain_p[...] = total.astype(BF)
+    over_p = copies.start(gain_p, gain_pp, place.peer())
+    over_p.wait_recv()
+    gains_out[...] = gain_p[...].astype(F32) + gain_pp[...].astype(F32)
+    for cols, second_a, second_b in second:
+        for half in range(2):
+            out[pl.ds(half * 32, 32), cols] = second_a.total(half)
+            out[pl.ds(64 + half * 32, 32), cols] = second_b.total(half)
+    copies.finish()
+
+
+def seq_reduce(grads, gains):
+    grads = grads.reshape(4, 4, 128, COLS)
+    gains = gains.reshape(4, 4, 16, HD)
+    bufs = []
+    for at, width in SPLITS:
+        bufs += [pltpu.VMEM((2, 4, 32, width), BF)] * 8
+        bufs += [pltpu.VMEM((4, 2, 32, width), BF)] * 2
+    for at, width in SPLITS:
+        bufs += [pltpu.VMEM((2, 32, width), BF)] * 8
+    bufs += [
+        pltpu.VMEM((3, 4, 16, HD), BF),
+        pltpu.VMEM((4, 16, HD), BF),
+        pltpu.VMEM((3, 16, HD), BF),
+        pltpu.VMEM((16, HD), BF),
+        pltpu.VMEM((3, 16, HD), BF),
+        pltpu.VMEM((16, HD), BF),
+        pltpu.VMEM((16, HD), BF),
+    ]
+    count = len(SPLITS) * 24 + 10
+    return call(
+        seq_kernel,
+        (shape((128, COLS), F32), shape((16, HD), F32)),
+        bufs + [pltpu.SemaphoreType.DMA((count,)), pltpu.SemaphoreType.DMA((count,))],
+        5,
+        grads,
+        gains,
+    )
 
 
 def shifted(shard, axis, by):
@@ -61,25 +534,6 @@
         ],
         axis=-1,
     )
-
-
-def join_pair(earlier, later):
-    early_state, early_norm, early_key = earlier
-    late_state, late_norm, late_key = later
-    same_key = ((early_key == late_key) | (late_key < 0.0)).astype(jnp.float32)
-    return (
-        late_state + same_key[..., None, None] * early_state,
-        late_norm + same_key[..., None] * early_norm,
-        jnp.where(late_key < 0.0, early_key, late_key),
-    )
-
-
-def forward_sum(partial_sum):
-    return lax.psum(partial_sum.astype(jnp.bfloat16), "mp").astype(jnp.float32)
-
-
-def backward_sum(partial_sum):
-    return lax.psum(partial_sum.astype(jnp.bfloat16), "mp").astype(jnp.float32)
 
 
 def weight_grad(left_rows, right_rows):
@@ -114,8 +568,6 @@
     heads_win = win_query.shape[1] // HD
     inputs = tokens.astype(jnp.float32)
     group_float = group_ids.astype(jnp.float32)
-    first_key = group_float[0:1]
-    last_key = group_float[row_count - 1 :]
     positions = jnp.arange(row_count)
     causal_mask = (
         (positions[None, :] <= positions[:, None]) & (group_ids[None, :] == group_ids[:, None])
@@ -149,16 +601,8 @@
         preferred_element_type=jnp.float32,
     )
     local_norm = jnp.sum(key_full * last_group[:, None, None], axis=0)
-    empty_state = jnp.zeros_like(local_state)
-    empty_norm = jnp.zeros_like(local_norm)
-    no_key = -jnp.ones((1,), jnp.float32)
-    carried_state, carried_norm, prev_key = entering(
-        (local_state, local_norm, last_key),
-        "seq",
-        join_pair,
-        (empty_state, empty_norm, no_key),
-        False,
-    )
+    carried_state, carried_norm = state_scan(local_state, local_norm, False)
+    prev_key = jnp.where(lax.axis_index("seq") > 0, group_float[0:1], -1.0)
     incoming = (group_float == prev_key[0]).astype(jnp.float32)
     numerator = jnp.einsum(
         "hij,jhd->ihd", kernel_low, value_lin, preferred_element_type=jnp.float32
@@ -170,10 +614,12 @@
     ] * jnp.einsum("ihf,hf->ih", query_full, carried_norm, precision=PRECISE)
     quotient = numerator / denominator[:, :, None]
     mixed_lin = quotient.astype(jnp.bfloat16).reshape(row_count, heads_lin * HD)
-    resid_one = inputs + forward_sum(
-        jnp.dot(mixed_lin, lin_output, preferred_element_type=jnp.float32)
-    )
-    normed_two = normalize(resid_one, gain_two).astype(jnp.bfloat16)
+    own_at = (lax.axis_index("mp") % 2) * HALF_ROWS + (lax.axis_index("mp") // 2) * OWN
+    own_tokens = lax.dynamic_slice_in_dim(tokens, own_at, OWN, 0).astype(F32)
+    own_out_grad = lax.dynamic_slice_in_dim(out_grad, own_at, OWN, 0).astype(F32)
+    normed_two, resid_one = mp_forward(
+        jnp.dot(mixed_lin, lin_output, preferred_element_type=jnp.float32), own_tokens, gain_two
+    )
     query_win = (
         jnp.dot(normed_two, win_query, preferred_element_type=jnp.float32)
         .astype(jnp.bfloat16)
@@ -219,17 +665,14 @@
         .astype(jnp.bfloat16)
         .reshape(row_count, heads_win * HD)
     )
-    resid_two = resid_one + forward_sum(
-        jnp.dot(mixed_win, win_output, preferred_element_type=jnp.float32)
-    )
-    normed_three = normalize(resid_two, gain_three).astype(jnp.bfloat16)
+    normed_three, resid_two = mp_forward(
+        jnp.dot(mixed_win, win_output, preferred_element_type=jnp.float32), resid_one, gain_three
+    )
     gate_act = jnp.dot(normed_three, mlp_gate, preferred_element_type=jnp.float32)
     up_act = jnp.dot(normed_three, mlp_up, preferred_element_type=jnp.float32)
     hidden = (jax.nn.silu(gate_act) * up_act).astype(jnp.bfloat16)
-    result = (
-        resid_two + forward_sum(jnp.dot(hidden, mlp_down, preferred_element_type=jnp.float32))
-    ).astype(jnp.bfloat16)
-    down_grad = weight_grad(hidden, out_grad)
+    result = mp_plain(jnp.dot(hidden, mlp_down, preferred_element_type=jnp.float32), resid_two)
+    down_grad = weight_grad(out_grad, hidden)
     hidden_grad = input_grad(out_grad, mlp_down)
     act_value, act_back = jax.vjp(
         lambda gate_in, up_in: jax.nn.silu(gate_in) * up_in, gate_act, up_act
@@ -239,12 +682,13 @@
     up_low = up_grad.astype(jnp.bfloat16)
     gate_wgrad = weight_grad(normed_three, gate_low)
     up_wgrad = weight_grad(normed_three, up_low)
-    normed_grad = backward_sum(input_grad(gate_low, mlp_gate) + input_grad(up_low, mlp_up))
-    norm_value, norm_back = jax.vjp(normalize, resid_two, gain_three)
-    resid_grad, gain_three_grad = norm_back(normed_grad)
-    grad_two = out_grad.astype(jnp.float32) + resid_grad
-    win_low = grad_two.astype(jnp.bfloat16)
-    win_output_grad = weight_grad(mixed_win, win_low)
+    win_low, grad_two, gain_three_grad = mp_backward(
+        input_grad(gate_low, mlp_gate) + input_grad(up_low, mlp_up),
+        resid_two,
+        gain_three,
+        own_out_grad,
+    )
+    win_output_grad = weight_grad(win_low, mixed_win)
     mixed_grad = (
         input_grad(win_low, win_output).astype(jnp.bfloat16).reshape(row_count, heads_win, HD)
     )
@@ -276,16 +720,15 @@
     win_query_grad = weight_grad(normed_two, query_win_low)
     win_key_grad = weight_grad(normed_two, key_win_low)
     win_value_grad = weight_grad(normed_two, value_win_low)
-    normed_grad_two = backward_sum(
+    lin_low, grad_one, gain_two_grad = mp_backward(
         input_grad(query_win_low, win_query)
         + input_grad(key_win_low, win_key)
-        + input_grad(value_win_low, win_value)
-    )
-    norm_value_two, norm_back_two = jax.vjp(normalize, resid_one, gain_two)
-    resid_grad_two, gain_two_grad = norm_back_two(normed_grad_two)
-    grad_one = grad_two + resid_grad_two
-    lin_low = grad_one.astype(jnp.bfloat16)
-    lin_output_grad = weight_grad(mixed_lin, lin_low)
+        + input_grad(value_win_low, win_value),
+        resid_one,
+        gain_two,
+        grad_two,
+    )
+    lin_output_grad = weight_grad(lin_low, mixed_lin)
     mix_grad = (
         lax.optimization_barrier(input_grad(lin_low, lin_output).astype(jnp.bfloat16))
         .astype(jnp.float32)
@@ -316,16 +759,7 @@
     query_used = query_full * incoming[:, None, None]
     state_in_grad = jnp.einsum("ihf,ihd->hfd", query_used, numer_grad, precision=PRECISE)
     norm_in_grad = jnp.einsum("ihf,ih->hf", query_used, denom_grad, precision=PRECISE)
-    later_state, later_norm, later_key = entering(
-        (state_in_grad, norm_in_grad, first_key),
-        "seq",
-        join_pair,
-        (empty_state, empty_norm, no_key),
-        True,
-    )
-    owned_mask = (later_key == last_key).astype(jnp.float32)[0]
-    summary_state = owned_mask * later_state
-    summary_norm = owned_mask * later_norm
+    summary_state, summary_norm = state_scan(state_in_grad, norm_in_grad, True)
     key_feat_grad = key_feat_grad + last_group[:, None, None] * (
         jnp.einsum("jhd,hfd->jhf", value_full, summary_state, precision=PRECISE)
         + summary_norm[None]
@@ -343,61 +777,56 @@
     lin_query_grad = weight_grad(normed_one, query_low)
     lin_key_grad = weight_grad(normed_one, key_low)
     lin_value_grad = weight_grad(normed_one, value_low)
-    normed_grad_one = backward_sum(
+    tokens_low, tokens_grad_own, gain_one_grad = mp_backward(
         input_grad(query_low, lin_query)
         + input_grad(key_low, lin_key)
-        + input_grad(value_low, lin_value)
-    )
-    norm_value_one, norm_back_one = jax.vjp(normalize, inputs, gain_one)
-    resid_grad_one, gain_one_grad = norm_back_one(normed_grad_one)
-    tokens_grad = grad_one + resid_grad_one
-    reduced = tuple(
-        (
-            lax.psum_scatter(
-                gain_one_grad.astype(jnp.bfloat16), "seq", scatter_dimension=0, tiled=True
-            ).astype(jnp.float32),
-            lax.psum_scatter(
-                lin_query_grad.astype(jnp.bfloat16), "seq", scatter_dimension=0, tiled=True
-            ).astype(jnp.float32),
-            lax.psum_scatter(
-                lin_key_grad.astype(jnp.bfloat16), "seq", scatter_dimension=0, tiled=True
-            ).astype(jnp.float32),
-            lax.psum_scatter(
-                lin_value_grad.astype(jnp.bfloat16), "seq", scatter_dimension=0, tiled=True
-            ).astype(jnp.float32),
-            lax.psum_scatter(
-                lin_output_grad.astype(jnp.bfloat16), "seq", scatter_dimension=1, tiled=True
-            ).astype(jnp.float32),
-            lax.psum_scatter(
-                gain_two_grad.astype(jnp.bfloat16), "seq", scatter_dimension=0, tiled=True
-            ).astype(jnp.float32),
-            lax.psum_scatter(
-                win_query_grad.astype(jnp.bfloat16), "seq", scatter_dimension=0, tiled=True
-            ).astype(jnp.float32),
-            lax.psum_scatter(
-                win_key_grad.astype(jnp.bfloat16), "seq", scatter_dimension=0, tiled=True
-            ).astype(jnp.float32),
-            lax.psum_scatter(
-                win_value_grad.astype(jnp.bfloat16), "seq", scatter_dimension=0, tiled=True
-            ).astype(jnp.float32),
-            lax.psum_scatter(
-                win_output_grad.astype(jnp.bfloat16), "seq", scatter_dimension=1, tiled=True
-            ).astype(jnp.float32),
-            lax.psum_scatter(
-                gain_three_grad.astype(jnp.bfloat16), "seq", scatter_dimension=0, tiled=True
-            ).astype(jnp.float32),
-            lax.psum_scatter(
-                gate_wgrad.astype(jnp.bfloat16), "seq", scatter_dimension=0, tiled=True
-            ).astype(jnp.float32),
-            lax.psum_scatter(
-                up_wgrad.astype(jnp.bfloat16), "seq", scatter_dimension=0, tiled=True
-            ).astype(jnp.float32),
-            lax.psum_scatter(
-                down_grad.astype(jnp.bfloat16), "seq", scatter_dimension=1, tiled=True
-            ).astype(jnp.float32),
-        )
-    )
-    return (result, tokens_grad) + reduced
+        + input_grad(value_low, lin_value),
+        own_tokens,
+        gain_one,
+        grad_one,
+    )
+    grads = jnp.concatenate(
+        [
+            part.astype(BF)
+            for part in (
+                lin_query_grad,
+                lin_key_grad,
+                lin_value_grad,
+                lin_output_grad,
+                win_query_grad,
+                win_key_grad,
+                win_value_grad,
+                win_output_grad,
+                gate_wgrad,
+                up_wgrad,
+                down_grad,
+            )
+        ],
+        axis=1,
+    )
+    gains = jnp.concatenate([gain_one_grad, gain_two_grad, gain_three_grad]).reshape(3, 16, HD)
+    gains = jnp.pad(jnp.transpose(gains, (1, 0, 2)), ((0, 0), (0, 13), (0, 0))).astype(BF)
+    sums, gain_sums = seq_reduce(grads, gains)
+    cuts = [0, 32, 64, 320, 576, 832, 1088, 1344, 1600, 2304, 3008, 3712]
+    pieces = [sums[:, a:b] for a, b in zip(cuts[:-1], cuts[1:])]
+    return (
+        result,
+        tokens_low.astype(F32),
+        gain_sums[0],
+        pieces[0],
+        pieces[1],
+        pieces[2],
+        pieces[3].T,
+        gain_sums[1],
+        pieces[4],
+        pieces[5],
+        pieces[6],
+        pieces[7].T,
+        gain_sums[2],
+        pieces[8],
+        pieces[9],
+        pieces[10].T,
+    )
 
 
 def solution(mesh):

time: 1510 us -> 568 us (0.38)
  waiting for transfers between devices: 924 us -> 0.01 us
  Pallas kernels: 0 us -> 322 us
  blocking collectives: 163 us -> 0 us
  other arithmetic: 108 us -> 24.7 us
  loops' own time: 63.7 us -> 0 us
  local copies, waits for them, and re-layouts: 87.6 us -> 67.9 us
    unnamed x25 -> x0, waiting for transfers between devices: 377 us -> none
    psum x5 -> x0, waiting for transfers between devices: 329 us -> none  [the longest x3 196 us: forward_sum(): return lax.psum(partial_sum.astype(jnp.bfloat16), 'mp').astype(jnp.float32)]
    pallas_call x0 -> x9, Pallas kernels: none -> 322 us  [call(): pl.pallas_call(kernel, out_shape=outs, in_specs=vmem(len(args)), out_spec...]
    reduce_scatter x4 -> x0, waiting for transfers between devices: 217 us -> none  [the longest x1 74.1 us: local(): lax.psum_scatter(win_value_grad.astype(jnp.bfloat16), 'seq', scatter_dime...]
    unnamed x2 -> x0, blocking collectives: 118 us -> none
    another operation x2 -> x0, loops' own time: 63.7 us -> none  [entering(): return lax.fori_loop(0, size, turn, start)]
    all_gather x2 -> x0, blocking collectives: 45.8 us -> none  [entering(): lax.all_gather(part.astype(kind), axis)]
    select_n x64 -> x0, other arithmetic: 45.4 us -> none  [turn(): return jax.tree.map(lambda a, b: jnp.where(reached, a, b), new, before)]
  transfers between devices with their start and end apart: 23 -> 5, of which waited for: 15 -> 0; matrix products, arithmetic and copies ran while one was open for 13% -> 4% of each run, Pallas kernels for 0% -> 5%
where the time goes in v1:
time: 568 us; the launch traced here: 556 us
  Pallas kernels  322 us (57%)
  matrix products  126 us (22%)
  local copies, waits for them, and re-layouts  67.9 us (12%)
  other arithmetic  24.7 us (4%)
  starting transfers between devices  13.2 us (2%)
    pallas_call x9, Pallas kernels, call(): pl.pallas_call(kernel, out_shape=outs, in_specs=vmem(len(args)), out_spec...  322 us
    dot_general x11, matrix products, input_grad(): jnp.einsum('tb,ab->ta', right_rows, weight_mat, preferred_element_type=jn...  42.9 us
    dot_general x11, matrix products, weight_grad(): jnp.einsum('ta,tb->ab', left_rows, right_rows, preferred_element_type=jnp...  22.3 us
    concatenate x1, local copies, waits for them, and re-layouts, local(): jnp.concatenate([part.astype(BF) for part in (lin_query_grad, lin_key_gra...  19.3 us
    unnamed x174, local copies, waits for them, and re-layouts  18.8 us
    ppermute x5, starting transfers between devices, shifted(): return lax.ppermute(shard, axis, pairs)  13.2 us
  transfers between devices with their start and end apart: 5, of which 0 were waited for; matrix products, arithmetic and copies ran while one was open for 4% of the time, Pallas kernels for 5%

profile of v1, /device:TPU:0, one launch (start us, length us, event | category | flops | bytes accessed | tf_op | source)
XLA Modules:
  0.0 556.5 jit_solution(16349804847118703536)
XLA Ops:
  2.9 1.9 fusion.38
  4.8 2.1 fusion.1
  13.8 2.1 convolution_convert_fusion.21
  19.5 22.4 %shard_map.288 = f32[576,128]{1,0:T(8,128)} custom-call(bf16[576,128]{1,0:T(8,128)(2,1)} %fusion.51.state), custom_call_target="tpu_custom_call" | custom-call | tf_op jit(solution)/shard_map/pallas_call | solution.py:238
  42.5 1.7 slice.148
  44.9 2.4 multiply_convert_fusion.8
  49.1 2.4 convert_reduce_fusion
  51.5 1.7 reshape.381
  53.2 1.7 convolution_multiply_fusion.3
  55.6 2.5 fusion.67
  58.8 2.1 convolution_convert_fusion.4.part
  60.8 2.1 dynamic-slice_convert_fusion
  62.9 30.2 %shard_map.289 = (bf16[512,2048]{1,0:T(8,128)(2,1)}, f32[64,2048]{1,0:T(8,128)}) custom-call(bf16[512,2048]{1,0:T(8,128)(2,1)} %convolution_convert_fusion.4.part, f32[64,2048]{1,0:T(8,128)} %get-tuple-element.137.resid, f32[1,2048]{1,0:T(1,128)} %bitcast.266), custom_call_target="tpu_custom_call" | custom-call | tf_op jit(solution)/shard_map/pallas_call | solution.py:238
  93.2 2.7 convolution_convert_fusion.17
  96.5 3.9 collective-permute-start.2
  101.0 2.1 collective-permute-start.1
  104.6 4.5 collective-permute-start
  114.0 1.9 fusion.34
  117.3 1.7 bitcast_dynamic-update-slice_fusion
  120.3 1.7 bitcast_dynamic-update-slice_fusion.1
  122.0 4.2 fusion.68
  126.2 3.3 convolution_convert_fusion.16
  129.5 3.4 convolution_convert_fusion.3.part
  132.9 29.3 %shard_map.290 = (bf16[512,2048]{1,0:T(8,128)(2,1)}, f32[64,2048]{1,0:T(8,128)}) custom-call(bf16[512,2048]{1,0:T(8,128)(2,1)} %convolution_convert_fusion.3.part, f32[64,2048]{1,0:T(8,128)} %get-tuple-element.55.resid, f32[1,2048]{1,0:T(1,128)} %bitcast.264), custom_call_target="tpu_custom_call" | custom-call | tf_op jit(solution)/shard_map/pallas_call | solution.py:238
  162.2 4.3 fusion.70
  166.5 1.7 fusion.71
  168.2 3.1 multiply_convert_fusion.3
  171.4 1.8 fusion.72
  173.2 15.7 %add_convert_fusion.2.part = bf16[512,2048]{1,0:T(8,128)(2,1)} fusion(f32[512,2048]{1,0:T(8,128)S(1)} %fusion.72, bf16[512,704]{0,1:T(8,128)(2,1)S(1)} %get-tuple-element.106, bf16[2048,704]{0,1:T(8,128)(2,1)S(1)} %copy-done.71), kind=kOutput, calls=%fused_computation.8 | convolution fusion | flops 1478492160 | bytes 9895936 | tf_op jit(solution)/shard_map/tb,ab->ta/dot_general | solution.py:544
  188.9 29.3 %shard_map.292 = (bf16[512,2048]{1,0:T(8,128)(2,1)}, f32[64,2048]{1,0:T(8,128)}, f32[1,2048]{1,0:T(1,128)}) custom-call(bf16[512,2048]{1,0:T(8,128)(2,1)} %add_convert_fusion.2.part, f32[64,2048]{1,0:T(8,128)} %get-tuple-element.57.resid, f32[1,2048]{1,0:T(1,128)} %bitcast.265, f32[64,2048]{1,0:T(8,128)} %get-tuple-element.136.grad), custom_call_target="tpu_custom_call" | custom-call | tf_op jit(solution)/shard_map/pallas_call | solution.py:238
  218.1 3.3 convolution_convert_fusion.15
  221.5 3.3 convolution_bitcast_fusion.2
  224.8 2.5 multiply_reduce_fusion
  233.7 3.2 convolution_convert_fusion.5.part
  236.9 2.8 fusion.73
  240.4 30.2 %shard_map.291 = bf16[512,2048]{1,0:T(8,128)(2,1)} custom-call(bf16[512,2048]{1,0:T(8,128)(2,1)} %convolution_convert_fusion.5.part, f32[64,2048]{1,0:T(8,128)} %get-tuple-element.57.resid), custom_call_target="tpu_custom_call" | custom-call | tf_op jit(solution)/shard_map/pallas_call | solution.py:238
  275.4 2.1 add_convert_fusion.1.part
  277.4 28.8 %shard_map.293 = (bf16[512,2048]{1,0:T(8,128)(2,1)}, f32[64,2048]{1,0:T(8,128)}, f32[1,2048]{1,0:T(1,128)}) custom-call(bf16[512,2048]{1,0:T(8,128)(2,1)} %add_convert_fusion.1.part, f32[64,2048]{1,0:T(8,128)} %get-tuple-element.55.resid, f32[1,2048]{1,0:T(1,128)} %bitcast.267, f32[64,2048]{1,0:T(8,128)} %get-tuple-element.59.grad), custom_call_target="tpu_custom_call" | custom-call | tf_op jit(solution)/shard_map/pallas_call | solution.py:238
  306.3 2.4 convolution_convert_fusion.14
  312.4 23.5 %shard_map.294 = f32[576,128]{1,0:T(8,128)} custom-call(bf16[576,128]{1,0:T(8,128)(2,1)} %fusion.52.state), custom_call_target="tpu_custom_call" | custom-call | tf_op jit(solution)/shard_map/pallas_call | solution.py:238
  335.9 1.7 slice.162
  340.4 1.9 fusion.24
  345.6 2.7 fusion.75
  348.3 1.7 reshape.402
  351.3 2.0 convolution_multiply_fusion.2
  353.3 1.7 fusion.25
  355.0 1.7 fusion.21
  358.5 2.8 fusion.76
  362.4 1.7 fusion.8
  364.1 1.7 fusion.9
  365.8 1.7 fusion.10
  367.5 1.7 fusion.11
  369.2 1.7 fusion.12
  370.9 1.7 fusion.13
  373.0 3.3 fusion.4
  376.3 3.3 fusion.5
  379.6 3.3 fusion.7
  382.9 19.3 %copy.84 = bf16[2048,3712]{1,0:T(8,128)(2,1)} copy(bf16[2048,3712]{0,1:T(8,128)(2,1)} %fusion.7) | data formatting | bytes 30408704 | tf_op jit(solution)/shard_map/concatenate | solution.py:788
  402.2 5.5 add_convert_fusion.part
  407.7 30.3 %shard_map.295 = (bf16[512,2048]{1,0:T(8,128)(2,1)}, f32[64,2048]{1,0:T(8,128)}, f32[1,2048]{1,0:T(1,128)}) custom-call(bf16[512,2048]{1,0:T(8,128)(2,1)} %add_convert_fusion.part, f32[64,2048]{1,0:T(8,128)} %get-tuple-element.137.resid, f32[1,2048]{1,0:T(1,128)} %bitcast.268, f32[64,2048]{1,0:T(8,128)} %get-tuple-element.61.grad), custom_call_target="tpu_custom_call" | custom-call | tf_op jit(solution)/shard_map/pallas_call | solution.py:238
  439.4 98.1 %shard_map.296 = (f32[128,3712]{1,0:T(8,128)}, f32[16,128]{1,0:T(8,128)}) custom-call(bf16[4,4,128,3712]{3,2,1,0:T(8,128)(2,1)} %bitcast.221, bf16[4,4,16,128]{3,2,1,0:T(8,128)(2,1)} %bitcast.255), custom_call_target="tpu_custom_call" | custom-call | tf_op jit(solution)/shard_map/pallas_call | solution.py:238
  539.0 2.5 slice_bitcast_fusion.1
  541.5 1.6 fusion.66
  550.9 2.5 convert_element_type.246
  (255 shorter events, 66.0 us)
Async XLA Ops:
  0.6 167.6 %copy-start = (bf16[704,2048]{1,0:T(8,128)(2,1)S(1)}, bf16[704,2048]{1,0:T(8,128)(2,1)}, u32[]{:S(2)}) copy-start(bf16[704,2048]{1,0:T(8,128)(2,1)} %param.36) | copy-start | bytes 8650756
  0.7 6.3 %copy-start.5 = (bf16[512,2048]{1,0:T(8,128)(2,1)S(1)}, bf16[512,2048]{1,0:T(8,128)(2,1)}, u32[]{:S(2)}) copy-start(bf16[512,2048]{1,0:T(8,128)(2,1)} %param.21) | copy-start | bytes 6291460
  0.7 6.3 %copy-start.52 = (f32[2048]{0:T(1024)S(1)}, f32[2048]{0:T(1024)}, u32[]{:S(2)}) copy-start(f32[2048]{0:T(1024)} %param.23) | copy-start | bytes 24580
  1.5 9.8 %copy-start.59 = (f32[512]{0:T(512)}, f32[512]{0:T(512)S(1)}, u32[]{:S(2)}) copy-start(f32[512]{0:T(512)S(1)} %convert_element_type.205) | copy-start | bytes 6148
  7.9 3.5 copy-start.2
  7.9 2.0 copy-start.33
  8.6 3.9 copy-start.53
  9.8 7.6 %copy-start.8 = (bf16[512,2,16,16]{0,3,2,1:T(8,128)(2,1)}, bf16[512,2,16,16]{0,3,2,1:T(8,128)(2,1)S(1)}, u32[]{:S(2)}) copy-start(bf16[512,2,16,16]{0,3,2,1:T(8,128)(2,1)S(1)} %multiply_convert_fusion.5) | copy-start | bytes 1572868
  13.7 3.7 copy-start.69
  13.7 30.5 %copy-start.58 = (f32[512]{0:T(512)}, f32[512]{0:T(512)S(1)}, u32[]{:S(2)}) copy-start(f32[512]{0:T(512)S(1)} %get-tuple-element.105) | copy-start | bytes 6148
  13.7 30.5 %copy-start.60 = (bf16[273]{0:T(512)(128)(2,1)}, bf16[273]{0:T(512)(128)(2,1)S(1)}, u32[]{:S(2)}) copy-start(bf16[273]{0:T(512)(128)(2,1)S(1)} %pad.42.clone) | copy-start | bytes 1642
  42.5 4.9 copy-start.51
  44.9 3.1 copy-start.61
  44.9 3.3 copy-start.65
  44.9 4.2 copy-start.9
  44.9 4.2 copy-start.11
  53.2 5.6 %copy-start.28 = (bf16[256,2048]{1,0:T(8,128)(2,1)S(1)}, bf16[256,2048]{1,0:T(8,128)(2,1)}, u32[]{:S(2)}) copy-start(bf16[256,2048]{1,0:T(8,128)(2,1)} %param.27) | copy-start | bytes 3145732
  55.6 2.5 copy-start.49
  93.1 7.3 %copy-start.70 = (bf16[512]{0:T(512)(128)(2,1)S(1)}, bf16[512]{0:T(512)(128)(2,1)}, u32[]{:S(2)}) copy-start(bf16[512]{0:T(512)(128)(2,1)} %copy-done.69) | copy-start | bytes 3076
  93.1 10.0 %copy-start.23 = (bf16[2048,256]{1,0:T(8,128)(2,1)S(1)}, bf16[2048,256]{1,0:T(8,128)(2,1)}, u32[]{:S(2)}) copy-start(bf16[2048,256]{1,0:T(8,128)(2,1)} %param.31) | copy-start | bytes 3145732
  93.2 10.0 %copy-start.72 = (bf16[512,2048]{1,0:T(8,128)(2,1)S(1)}, bf16[512,2048]{1,0:T(8,128)(2,1)}, u32[]{:S(2)}) copy-start(bf16[512,2048]{1,0:T(8,128)(2,1)} %get-tuple-element.54) | copy-start | bytes 6291460
  95.9 8.0 %copy-start.44 = (bf16[512,256]{1,0:T(8,128)(2,1)}, bf16[512,256]{1,0:T(8,128)(2,1)S(1)}, u32[]{:S(2)}) copy-start(bf16[512,256]{1,0:T(8,128)(2,1)S(1)} %convolution_convert_fusion.17) | copy-start | bytes 786436
  95.9 13.3 %copy-start.30 = (bf16[2048,256]{1,0:T(8,128)(2,1)S(1)}, bf16[2048,256]{1,0:T(8,128)(2,1)}, u32[]{:S(2)}) copy-start(bf16[2048,256]{1,0:T(8,128)(2,1)} %param.29) | copy-start | bytes 3145732
  96.5 19.3 %collective-permute-start.2 = (bf16[64,2,128]{2,0,1:T(8,128)(2,1)}, bf16[64,2,128]{2,0,1:T(8,128)(2,1)}, u32[]{:S(2)}, u32[]{:S(2)}) collective-permute-start(bf16[64,2,128]{2,0,1:T(8,128)(2,1)} %copy_bitcast_fusion), channel_id=1, source_target_pairs={{0,8},{8,16},{16,24},{24,32},{32,40},{40,48},{48,56},{56,64},{64,7... | collective-permute-start | bytes 98312 | tf_op jit(solution)/shard_map/ppermute | solution.py:515
  101.0 11.6 %collective-permute-start.1 = (bf16[64]{0:T(256)(128)(2,1)}, bf16[64]{0:T(256)(128)(2,1)}, u32[]{:S(2)}, u32[]{:S(2)}) collective-permute-start(bf16[64]{0:T(256)(128)(2,1)} %slice.153), channel_id=1, source_target_pairs={{0,8},{8,16},{16,24},{24,32},{32,40},{40,48},{48,56},{56,64},{64,7... | collective-permute-start | bytes 392 | tf_op jit(solution)/shard_map/ppermute | solution.py:515
  104.6 14.3 %collective-permute-start = (bf16[64,2,128]{2,0,1:T(8,128)(2,1)}, bf16[64,2,128]{2,0,1:T(8,128)(2,1)}, u32[]{:S(2)}, u32[]{:S(2)}) collective-permute-start(bf16[64,2,128]{2,0,1:T(8,128)(2,1)} %copy_bitcast_fusion.1), channel_id=1, source_target_pairs={{0,8},{8,16},{16,24},{24,32},{32,40},{40,48},{48,56},{56,64},{64,7... | collective-permute-start | bytes 98312 | tf_op jit(solution)/shard_map/ppermute | solution.py:515
  162.2 4.3 copy-start.71
  162.2 4.3 copy-start.74
  168.2 3.1 copy-start.13
  171.3 1.9 copy-start.80
  224.8 2.6 copy-start.14
  224.8 2.6 copy-start.68
  228.3 2.1 copy-start.48
  228.3 5.3 copy-start.78
  228.8 10.9 %copy-start.22 = (f32[576,2,128]{2,0,1:T(8,128)}, f32[576,2,128]{2,0,1:T(8,128)S(1)}, u32[]{:S(2)}) copy-start(f32[576,2,128]{2,0,1:T(8,128)S(1)} %fusion.26) | copy-start | bytes 1769476
  230.4 6.5 %copy-start.20 = (bf16[2,128,512]{2,1,0:T(8,128)(2,1)}, bf16[2,128,512]{2,1,0:T(8,128)(2,1)S(1)}, u32[]{:S(2)}) copy-start(bf16[2,128,512]{2,1,0:T(8,128)(2,1)S(1)} %fusion.29) | copy-start | bytes 786436
  230.4 40.2 %collective-permute-start.4 = (bf16[64,2,128]{2,0,1:T(8,128)(2,1)S(1)}, bf16[64,2,128]{2,0,1:T(8,128)(2,1)S(1)}, u32[]{:S(2)}, u32[]{:S(2)}) collective-permute-start(bf16[64,2,128]{2,0,1:T(8,128)(2,1)S(1)} %slice.205), channel_id=1, source_target_pairs={{8,0},{16,8},{24,16},{32,24},{40,32},{48,40},{56,48},{64,56},{72,6... | collective-permute-start | bytes 98312 | tf_op jit(solution)/shard_map/ppermute | solution.py:515
  232.4 39.3 %collective-permute-start.3 = (bf16[64,2,128]{2,0,1:T(8,128)(2,1)}, bf16[64,2,128]{2,0,1:T(8,128)(2,1)}, u32[]{:S(2)}, u32[]{:S(2)}) collective-permute-start(bf16[64,2,128]{2,0,1:T(8,128)(2,1)} %slice.206), channel_id=1, source_target_pairs={{8,0},{16,8},{24,16},{32,24},{40,32},{48,40},{56,48},{64,56},{72,6... | collective-permute-start | bytes 98312 | tf_op jit(solution)/shard_map/ppermute | solution.py:515
  233.7 3.2 copy-start.31
  236.9 2.9 copy-start.67
  240.4 32.4 %copy-start.32 = (bf16[2048,256]{1,0:T(8,128)(2,1)S(1)}, bf16[2048,256]{1,0:T(8,128)(2,1)}, u32[]{:S(2)}) copy-start(bf16[2048,256]{1,0:T(8,128)(2,1)} %param.30) | copy-start | bytes 3145732
  271.6 1.9 copy-start.25
  272.8 2.3 copy-start.4
  272.8 2.6 copy-start.24
  277.4 28.9 %copy-start.29 = (bf16[256,2048]{1,0:T(8,128)(2,1)S(1)}, bf16[256,2048]{1,0:T(8,128)(2,1)}, u32[]{:S(2)}) copy-start(bf16[256,2048]{1,0:T(8,128)(2,1)} %param.27) | copy-start | bytes 3145732
  306.3 2.6 copy-start.41
  306.3 2.7 copy-start.50
  309.0 29.8 %copy-start.12 = (f32[512,512]{0,1:T(8,128)S(1)}, f32[512,512]{0,1:T(8,128)}, u32[]{:S(2)}) copy-start(f32[512,512]{0,1:T(8,128)} %fusion.38) | copy-start | bytes 3145732
  309.6 28.0 %copy-start.63 = (f32[512,2]{0,1:T(2,128)}, f32[512,2]{0,1:T(2,128)S(1)}, u32[]{:S(2)}) copy-start(f32[512,2]{0,1:T(2,128)S(1)} %negate_divide_fusion) | copy-start | bytes 12292
  338.8 3.4 copy-start.10
  338.8 3.4 copy-start.62
  340.4 1.9 copy-start.6
  343.1 2.5 copy-start.40
  370.9 2.1 copy-start.75
  373.0 3.3 copy-start.81
  376.3 3.3 copy-start.57
  376.3 3.3 copy-start.79
  382.9 19.3 %copy-start.43 = (bf16[2048,32]{0,1:T(8,128)(2,1)S(1)}, bf16[2048,32]{0,1:T(8,128)(2,1)}, u32[]{:S(2)}) copy-start(bf16[2048,32]{0,1:T(8,128)(2,1)} %param.25) | copy-start | bytes 393220
  407.7 31.0 %copy-start.66 = (f32[1,2048]{1,0:T(1,128)S(1)}, f32[1,2048]{1,0:T(1,128)}, u32[]{:S(2)}) copy-start(f32[1,2048]{1,0:T(1,128)} %get-tuple-element.64) | copy-start | bytes 24580
  407.7 31.0 %copy-start.55 = (bf16[1,2048]{1,0:T(2,128)(2,1)S(1)}, bf16[1,2048]{1,0:T(2,128)(2,1)}, u32[]{:S(2)}) copy-start(bf16[1,2048]{1,0:T(2,128)(2,1)} %convert.73) | copy-start | bytes 12292
  539.0 11.9 %copy-start.15 = (bf16[512,2048]{1,0:T(8,128)(2,1)S(1)}, bf16[512,2048]{1,0:T(8,128)(2,1)}, u32[]{:S(2)}) copy-start(bf16[512,2048]{1,0:T(8,128)(2,1)} %get-tuple-element.62) | copy-start | bytes 6291460
  544.1 4.8 copy-start.46
  550.9 2.5 copy-start.7
  553.5 2.6 copy-start.1
  (23 other events, 31.4 us)
